TPU v7x, 32 devices: a whole 2x2x4 slice. The times are simulated.
32 devices in a mesh: ens: 2 (over y), tile: 4 (over z), chan: 2 (over x), sec: 2 (over core).
Axes of the slice: x: 2, y: 2, z: 4, core: 2. Of those that a mesh axis runs over, the one named last changes fastest.
Arguments:
- ocean_state: bfloat16 [256, 128, 4, 128], P(('chan', 'sec'), ('ens', 'tile')), parts along dimension 1, may hold values from -6 to 6
- atmos: bfloat16 [16384, 384], P(('ens', 'tile')), parts along dimension 0, may hold values from -6 to 6
- flux_weight: bfloat16 [384, 256], P(None, ('chan', 'sec')), may hold values from -0.3125 to 0.3125
- conv_weight: bfloat16 [9, 256, 256], P(None, None, ('chan', 'sec')), may hold values from -0.125 to 0.125
- conv_bias: bfloat16 [256], P(('chan', 'sec')), may hold values from -3 to 3
- norm_gain: bfloat16 [256], P(('chan', 'sec')), may hold values from 0.5 to 2
- in_weight: bfloat16 [256, 1024], P(None, ('chan', 'sec')), may hold values from -0.375 to 0.375
- in_bias: bfloat16 [1024], P(('chan', 'sec')), may hold values from -3 to 3
- out_weight: bfloat16 [1024, 256], P(('chan', 'sec')), may hold values from -0.25 to 0.25
- layer_scale: bfloat16 [256], P(('chan', 'sec')), may hold values from 0.5 to 2
- cell_mask: int32 [64, 4, 128], P('tile'), may hold values from 0 to 1, as said below
- neighbours: int32 [64, 8], P('tile'), may hold values from -1 to 63, as said below
- remap: int32 [64, 4, 128], P('tile'), may hold values from 0 to 8191
Outputs:
- ocean_next: bfloat16 [256, 128, 4, 128], P(('chan', 'sec'), ('ens', 'tile')), parts along dimension 1
There are 2 independent parts, one for each index of `ens`. A program takes and returns all parts, laid end to end along the dimension named above; an argument that names none is the same for every part. Nothing has to cross between parts.
Inputs may be any that keep to these rules, and one draw needn't show every extreme that they name: `cell_mask`: land cells and every cell of a land block are 0. `neighbours`: for a slot among those of tile index t, each entry is -1 or a slot among those of tile indices t - 1, t and t + 1, i.e. in [(t - 1) * 16, (t + 2) * 16); entries that name land blocks are -1.
All inputs are finite; a program needn't handle non-finite values.
Results may differ from a plain program's by a relative error of at most 0.01.
Values may be sent and summed in bfloat16 or wider, within the bound.
No kernel may reach another device: no remote copies, remote signals or barrier semaphores. Data moves between devices by JAX's collectives and lax.ppermute only.
A program may use at most 64 MiB of HBM per device.

v0:
```python
import functools

import jax
import jax.numpy as jnp
from jax import lax
from jax.experimental import pallas as pl
from jax.experimental.pallas import tpu as pltpu
from jax.sharding import PartitionSpec as P

norm_eps = 1e-06
bf16 = jnp.bfloat16
f32 = jnp.float32
GROUP = ("chan", "sec")
BIAS_ROWS = 32
VMEM = pl.BlockSpec(memory_space=pltpu.VMEM)
SMEM = pl.BlockSpec(memory_space=pltpu.SMEM)
ANY = pl.BlockSpec(memory_space=pl.ANY)


def shape(dims, dtype=bf16):
    return jax.ShapeDtypeStruct(dims, dtype)


def params(mib=20):
    return pltpu.CompilerParams(vmem_limit_bytes=mib * 1024 * 1024)


def ein(a, b, dims):
    return lax.dot_general(a, b, (dims, ((), ())), preferred_element_type=f32)


def start_kernel(
    place_ref, state_ref, conv_ref, bias_ref, gain_ref, in_ref, in_bias_ref, out_ref, *refs
):
    xt_ref, strips_ref, pack_ref, part_ref, state_v, conv_v, in_v, out_v, sems = refs
    groups, chan_local, per, block_rows, block_cols = state_v.shape
    taps, _, channels = conv_v.shape
    hid_local = out_v.shape[0]
    copies = [
        pltpu.make_async_copy(conv_ref, conv_v, sems.at[groups]),
        pltpu.make_async_copy(in_ref, in_v, sems.at[groups + 1]),
        pltpu.make_async_copy(out_ref, out_v, sems.at[groups + 2]),
    ]
    for copy in copies:
        copy.start()
    loads = []
    for d in range(groups):
        loads.append(
            pltpu.make_async_copy(
                state_ref.at[:, pl.ds(d * per, per)], state_v.at[d], sems.at[d]
            )
        )
        loads[d].start()

    def widen(ref):
        rows = ref[...].astype(f32)
        row = jnp.concatenate([rows[k : k + 1] for k in range(rows.shape[0])], axis=1)
        if row.shape[1] == channels:
            return row
        return jnp.concatenate([row, jnp.zeros((1, channels - row.shape[1]), f32)], axis=1)

    rest = jnp.zeros((BIAS_ROWS - 3, channels), f32)
    biases = jnp.concatenate(
        [widen(bias_ref), widen(gain_ref), widen(in_bias_ref), rest], axis=0
    )
    at = taps * chan_local
    pack_ref[pl.ds(at + 2 * hid_local, BIAS_ROWS), :] = biases.astype(bf16)
    for copy in copies:
        copy.wait()
    for t in range(taps):
        pack_ref[pl.ds(t * chan_local, chan_local), :] = conv_v[t]
    pack_ref[pl.ds(at, hid_local), :] = in_v[...].astype(f32).T.astype(bf16)
    pack_ref[pl.ds(at + hid_local, hid_local), :] = out_v[...]
    part = part_ref.shape[0]
    part_ref[...] = pack_ref[pl.ds(pl.multiple_of(place_ref[1] * part, 16), part), :]

    lane = lax.broadcasted_iota(jnp.int32, (chan_local, block_cols), 1)
    cols = jnp.zeros((chan_local, block_cols), f32)
    for d in range(groups):
        loads[d].wait()
        for s in range(per):
            slot = d * per + s
            rows = jnp.swapaxes(state_v[d, :, s].astype(f32), 0, 1)
            packed = rows.astype(bf16)
            xt_ref[slot] = packed
            strips_ref[2 * slot] = packed[0]
            strips_ref[2 * slot + 1] = packed[block_rows - 1]
            for r in range(block_rows):
                spot = 2 * (block_rows * slot + r)
                turned = pltpu.roll(rows[r], spot + 1, 1)
                cols = jnp.where((lane == spot) | (lane == spot + 1), turned, cols)
    strips_ref[strips_ref.shape[0] - 1] = cols.astype(bf16)


def start_step(
    place, groups, state, conv_weight, conv_bias, norm_gain, in_weight, in_bias, out_weight
):
    chan_local, slot_count, block_rows, block_cols = state.shape
    per = slot_count // groups
    taps, channels, _ = conv_weight.shape
    hid_local = out_weight.shape[0]
    rows = taps * chan_local + 2 * hid_local + BIAS_ROWS
    return pl.pallas_call(
        start_kernel,
        out_shape=(
            shape((slot_count, block_rows, chan_local, block_cols)),
            shape((2 * slot_count + 1, chan_local, block_cols)),
            shape((rows, channels)),
            shape((rows // 2, channels)),
        ),
        in_specs=[SMEM, ANY, ANY, VMEM, VMEM, ANY, VMEM, ANY],
        out_specs=(VMEM,) * 4,
        scratch_shapes=[
            pltpu.VMEM((groups, chan_local, per, block_rows, block_cols), bf16),
            pltpu.VMEM((taps, chan_local, channels), bf16),
            pltpu.VMEM((channels, hid_local), bf16),
            pltpu.VMEM((hid_local, channels), bf16),
            pltpu.SemaphoreType.DMA((groups + 3,)),
        ],
        compiler_params=params(60),
        name="start_step",
    )(
        place,
        state,
        conv_weight.transpose(0, 2, 1),
        conv_bias.reshape(-1, min(128, chan_local)),
        norm_gain.reshape(-1, min(128, chan_local)),
        in_weight,
        in_bias.reshape(-1, min(128, hid_local)),
        out_weight,
    )


def send(piece, d, count):
    return lax.ppermute(piece, GROUP, [(i, i ^ d) for i in range(count)])


def trade(pieces):
    count = len(pieces)
    got = list(pieces)
    for d in list(range(count // 2, count)) + list(range(1, count // 2)):
        got[d] = send(pieces[d], d, count)
    return got


def unpack_kernel(chan_local, hid_local, starts_ref, *refs):
    *pieces, conv_ref, in_ref, out_ref, col_ref, hid_col_ref, all_ref = refs
    groups, rows, channels = all_ref.shape
    unit = min(rows, *(piece.shape[0] for piece in pieces))
    for n, piece in enumerate(pieces):
        for k in range(piece.shape[0] // unit):
            at = starts_ref[n] + k
            parts = rows // unit
            start = pl.multiple_of((at % parts) * unit, 16)
            all_ref[at // parts, pl.ds(start, unit), :] = piece[pl.ds(k * unit, unit), :]
    at = 9 * chan_local
    for j in range(groups):
        for t in range(9):
            conv_ref[pl.ds(j * chan_local, chan_local), pl.ds(t * channels, channels)] = all_ref[
                j, pl.ds(t * chan_local, chan_local), :
            ]
        in_ref[pl.ds(j * hid_local, hid_local), :] = all_ref[j, pl.ds(at, hid_local), :]
        biases = all_ref[j, pl.ds(at + 2 * hid_local, BIAS_ROWS), :].astype(f32)
        across = biases.T
        col_ref[pl.ds(j * chan_local, chan_local), :] = across[:chan_local]
        hid_col_ref[pl.ds(j * hid_local, hid_local), :] = across[:hid_local]
    outs = jnp.concatenate(
        [all_ref[j, pl.ds(at + hid_local, hid_local), :] for j in range(groups)], axis=0
    )
    out_ref[...] = outs.astype(f32).T.astype(bf16)


def unpack_weights(pieces, starts, groups, chan_local, hid_local):
    rows = sum(piece.shape[0] for piece in pieces) // groups
    channels = groups * chan_local
    hidden = groups * hid_local
    return pl.pallas_call(
        functools.partial(unpack_kernel, chan_local, hid_local),
        out_shape=(
            shape((channels, 9 * channels)),
            shape((hidden, channels)),
            shape((channels, hidden)),
            shape((channels, BIAS_ROWS), f32),
            shape((hidden, BIAS_ROWS), f32),
        ),
        in_specs=[SMEM] + [VMEM] * len(pieces),
        out_specs=(VMEM,) * 5,
        scratch_shapes=[pltpu.VMEM((groups, rows, channels), bf16)],
        compiler_params=params(),
        name="unpack_weights",
    )(starts, *pieces)


def swap(value, axis):
    return lax.ppermute(value, axis, [(0, 1), (1, 0)])


def exchange_weights(packed, part):
    if lax.axis_size("ens") != 2 or lax.axis_size("chan") != 2 or lax.axis_size("sec") != 2:
        whole = lax.all_gather(packed, GROUP, axis=0, tiled=True)
        return [whole], jnp.zeros((1,), jnp.int32)
    ens, chan, sec = (lax.axis_index(name) for name in ("ens", "chan", "sec"))
    near = swap(part, "chan")
    near, held = lax.optimization_barrier((near, packed))
    far = swap(near, "ens")
    other = swap(held, "sec")
    near_other = swap(near, "sec")
    far_other = swap(far, "sec")
    own = 2 * (2 * chan + sec)
    beside = 2 * (2 * chan + 1 - sec)
    across = 2 * (2 * (1 - chan) + sec)
    corner = 2 * (2 * (1 - chan) + 1 - sec)
    starts = [own, beside, across + ens, across + 1 - ens, corner + ens, corner + 1 - ens]
    return [packed, other, near, far, near_other, far_other], jnp.stack(starts)


def flux_kernel(atmos_ref, weight_ref, out_ref):
    rows, lanes = out_ref.shape
    chan_local, features = weight_ref.shape
    weight = weight_ref[...]
    total = jnp.zeros((rows, lanes), f32)
    for k in range(lanes // chan_local):
        parts = [weight if j == k else jnp.zeros_like(weight) for j in range(lanes // chan_local)]
        wide = jnp.concatenate(parts, axis=0)
        total = total + ein(atmos_ref[pl.ds(k * rows, rows), :], wide, ((1,), (1,)))
    out_ref[...] = total.astype(bf16)


def fluxes_of(atmos, flux_weight):
    side = 128 // flux_weight.shape[1]
    return pl.pallas_call(
        flux_kernel,
        out_shape=shape((atmos.shape[0] // side, 128)),
        in_specs=[VMEM, VMEM],
        out_specs=VMEM,
        compiler_params=params(),
        name="fluxes",
    )(atmos, flux_weight.T)


def onehot_kernel(at_ref, out_ref):
    spot = lax.broadcasted_iota(jnp.int32, out_ref.shape, 0)
    out_ref[...] = (spot == at_ref[...]).astype(f32).astype(bf16)


def onehot_of(at, rows):
    return pl.pallas_call(
        onehot_kernel,
        out_shape=shape((rows, at.shape[1])),
        in_specs=[VMEM],
        out_specs=VMEM,
        compiler_params=params(),
        name="onehot",
    )(at)


def rim_kernel(place_ref, entry_ref, chosen_ref, prev_ref, own_ref, next_ref, *refs):
    *rims, held, cols = refs
    tiles, chan_local, block_cols = own_ref.shape
    groups = len(rims)
    slot_count = (tiles - 1) // 2
    per = slot_count // groups
    ends = jnp.concatenate(
        [prev_ref[tiles - 1], own_ref[tiles - 1], next_ref[tiles - 1]], axis=1
    )
    picked = ein(ends, chosen_ref[...], ((1,), (0,))).astype(bf16)
    for k in range(cols.shape[0]):
        cols[k] = picked[:, k * block_cols : (k + 1) * block_cols]
    held[pl.ds(0, tiles)] = prev_ref[...]
    held[pl.ds(tiles, tiles)] = own_ref[...]
    held[pl.ds(2 * tiles, tiles)] = next_ref[...]
    held[3 * tiles] = jnp.zeros((chan_local, block_cols), bf16)
    for d in range(groups):
        group = jnp.bitwise_xor(place_ref[0], d)
        for s in range(per):
            rims[d][2 * s] = held[entry_ref[0, group * per + s]]
            rims[d][2 * s + 1] = held[entry_ref[1, group * per + s]]
        rims[d][2 * per] = cols[group * (16 * per) // block_cols]


def rim_places(neighbours, first_slot, block_rows):
    slot_count = neighbours.shape[0]
    tiles = 2 * slot_count + 1
    valid = neighbours >= 0
    slot = jnp.clip(neighbours - first_slot, 0, 3 * slot_count - 1)
    tile_of = slot // slot_count
    place = tile_of * tiles + 2 * (slot - tile_of * slot_count)
    entries = jnp.stack(
        [
            jnp.where(valid[:, 2], place[:, 2] + 1, 3 * tiles),
            jnp.where(valid[:, 3], place[:, 3], 3 * tiles),
        ]
    )
    base = jnp.where(valid, 2 * block_rows * slot, -4 * block_rows)
    last = 2 * (block_rows - 1)
    west = [base[:, 4] + last] + [base[:, 0] + 2 * r for r in range(block_rows)] + [base[:, 6]]
    east = [base[:, 5] + last] + [base[:, 1] + 2 * r for r in range(block_rows)] + [base[:, 7]]
    none = [jnp.full((slot_count,), -1, jnp.int32)] * (8 - block_rows - 2)
    at = jnp.stack(west + none + [e + 1 for e in east] + none, axis=1)
    return entries, at.reshape(1, slot_count * 16)


def rims_of(place, entries, chosen, strips_prev, strips, strips_next, groups):
    tiles, chan_local, block_cols = strips.shape
    per = (tiles - 1) // 2 // groups
    return pl.pallas_call(
        rim_kernel,
        out_shape=(shape((2 * per + 1, chan_local, block_cols)),) * groups,
        in_specs=[SMEM, SMEM, VMEM, VMEM, VMEM, VMEM],
        out_specs=(VMEM,) * groups,
        scratch_shapes=[
            pltpu.VMEM((3 * tiles + 1, chan_local, block_cols), bf16),
            pltpu.VMEM((chosen.shape[1] // block_cols, chan_local, block_cols), bf16),
        ],
        compiler_params=params(),
        name="rims",
    )(place, entries, chosen, strips_prev, strips, strips_next)


def block_kernel(groups, place_ref, *refs):
    body_ref, refs = refs[0], refs[1:]
    rims, refs = refs[:groups], refs[groups:]
    conv_ref, in_ref, out_ref, col_ref, hid_col_ref = refs[:5]
    updates, scratch = refs[5 : 5 + groups], refs[5 + groups :]
    _, per, block_rows, chan_local, block_cols = body_ref.shape
    channels = groups * chan_local
    hidden = in_ref.shape[0]
    me = place_ref[0]
    lane = lax.broadcasted_iota(jnp.int32, (chan_local, block_cols), 1)
    bias = col_ref[:, 0:1]
    gain = col_ref[:, 1:2]
    base = (me * (16 * per)) % block_cols
    rows = [
        pl.multiple_of(jnp.bitwise_xor(me, d) * chan_local, chan_local) for d in range(groups)
    ]
    rim_v, side_v = scratch[6:]
    for d in range(groups):
        source = jnp.bitwise_xor(me, d)
        rim_v[source] = rims[d][...]
        side_v[source] = pltpu.roll(rims[d][2 * per].astype(f32), block_cols - base, 1)
    for s in range(per):
        taken, hid, upd_v = scratch[3 * (s % 2) : 3 * (s % 2) + 3]
        for d in range(groups):
            for p in range(block_rows + 2):
                if p == 0:
                    mid = rim_v[d, 2 * s]
                elif p == block_rows + 1:
                    mid = rim_v[d, 2 * s + 1]
                else:
                    mid = body_ref[d, s, p - 1]
                wide = mid.astype(f32)
                spot = 16 * s + p
                left = jnp.where(
                    lane == 0,
                    pltpu.roll(side_v[d], (block_cols - spot) % block_cols, 1),
                    pltpu.roll(wide, 1, 1),
                ).astype(bf16)
                right = jnp.where(
                    lane == block_cols - 1,
                    pltpu.roll(side_v[d], (2 * block_cols - 1 - spot - 8) % block_cols, 1),
                    pltpu.roll(wide, block_cols - 1, 1),
                ).astype(bf16)
                for a in range(3):
                    i = p - a
                    if 0 <= i < block_rows:
                        for b, piece in enumerate((left, mid, right)):
                            taken[
                                3 * a + b,
                                pl.ds(d * chan_local, chan_local),
                                pl.ds(i * block_cols, block_cols),
                            ] = piece
        columns = taken[...].reshape(9 * channels, block_rows * block_cols)
        conv = ein(conv_ref[...], columns, ((1,), (0,))) + bias
        squares = jnp.sum(conv * conv, axis=0, keepdims=True)
        normed = (conv * lax.rsqrt(squares / channels + norm_eps) * gain).astype(bf16)
        step = min(hidden, 256)
        for h in range(0, hidden, step):
            pre = ein(in_ref[pl.ds(h, step), :], normed, ((1,), (0,)))
            pre = pre + hid_col_ref[pl.ds(h, step), 2:3]
            act = pre * (0.5 * lax.erf(pre * (0.5**0.5)) + 0.5)
            hid[pl.ds(h, step), :] = act.astype(bf16)
        upd_v[...] = ein(out_ref[...], hid[...], ((1,), (0,))).astype(bf16)
        for d in range(groups):
            for i in range(block_rows):
                updates[d][s, i] = upd_v[
                    pl.ds(rows[d], chan_local), pl.ds(i * block_cols, block_cols)
                ]


def block_step(place, bodies, rims, weights):
    groups, per, block_rows, chan_local, block_cols = bodies.shape
    channels = groups * chan_local
    hidden = weights[1].shape[0]
    cells = per * block_rows * block_cols
    return pl.pallas_call(
        functools.partial(block_kernel, groups),
        out_shape=(shape(bodies.shape[1:]),) * groups,
        in_specs=[SMEM] + [VMEM] * (groups + 6),
        out_specs=(VMEM,) * groups,
        scratch_shapes=[
            pltpu.VMEM((9, channels, block_rows * block_cols), bf16),
            pltpu.VMEM((hidden, block_rows * block_cols), bf16),
            pltpu.VMEM((channels, block_rows * block_cols), bf16),
        ]
        * 2
        + [
            pltpu.VMEM((groups,) + rims[0].shape, bf16),
            pltpu.VMEM((groups, chan_local, block_cols), f32),
        ],
        compiler_params=params(24),
        cost_estimate=pl.CostEstimate(
            flops=2 * cells * (9 * channels * channels + 2 * channels * hidden),
            bytes_accessed=8 * 1024 * 1024,
            transcendentals=0,
        ),
        name="block_step",
    )(place, bodies, *rims, *weights)


def forcing_kernel(row_ref, side_ref, wide, out_ref, even, odd):
    slot_count, block_rows, chan_local, block_cols = out_ref.shape
    lanes = wide.shape[2]
    row_at = lax.broadcasted_iota(jnp.int32, (lanes, lanes), 0)
    col_at = lax.broadcasted_iota(jnp.int32, (lanes, lanes), 1)
    eye = (row_at == col_at).astype(f32).astype(bf16)
    count = slot_count * block_rows

    def fetch(q, got):
        for k in range(block_cols):
            got[pl.ds(k, 1), :] = wide[row_ref[q, k]]

    def emit(q, got):
        across = ein(eye, got[...].astype(bf16), ((1,), (1,)))
        side = side_ref[pl.ds(q, 1), :]
        total = across[:chan_local]
        for k in range(1, lanes // chan_local):
            total = jnp.where(side == k, across[k * chan_local : (k + 1) * chan_local], total)
        out_ref[q // block_rows, q % block_rows] = total.astype(bf16)

    fetch(0, even)

    def two(n, _):
        q = 2 * n
        fetch(q + 1, odd)
        emit(q, even)
        fetch(jnp.minimum(q + 2, count - 1), even)
        emit(q + 1, odd)
        return 0

    lax.fori_loop(0, count // 2, two, 0)


def gather_flux(flux):
    count = lax.axis_size("tile")
    if count > 4:
        whole = lax.all_gather(flux, "tile", axis=0)
        me = lax.axis_index("tile")
        return [jnp.take(whole, (me - d) % count, axis=0) for d in range(count)]
    pieces = [flux]
    for d in range(1, count):
        turn = [(i, (i + d) % count) for i in range(count)]
        pieces.append(lax.ppermute(flux, "tile", turn))
    return pieces


def forcing_of(pieces, remap, rows_local, chan_local):
    slot_count, block_rows, block_cols = remap.shape
    count = len(pieces)
    side_by = 128 // chan_local
    part = rows_local // side_by
    target = jnp.clip(remap, 0, count * rows_local - 1).reshape(-1, block_cols)
    tile_of = target // rows_local
    within = target - tile_of * rows_local
    side = within // part
    behind = lax.axis_index("tile") - tile_of
    behind = jnp.where(behind < 0, behind + count, behind)
    row = behind * part + within - side * part
    table = lax.optimization_barrier(jnp.concatenate(pieces, axis=0).astype(f32))[:, None, :]
    return pl.pallas_call(
        forcing_kernel,
        out_shape=shape((slot_count, block_rows, chan_local, block_cols)),
        in_specs=[SMEM, VMEM, VMEM],
        out_specs=VMEM,
        scratch_shapes=[pltpu.VMEM((block_cols, 128), f32)] * 2,
        compiler_params=params(),
        cost_estimate=pl.CostEstimate(
            flops=0, bytes_accessed=32 * 1024 * 1024, transcendentals=0
        ),
        name="forcing",
    )(row, side, table)


def final_kernel(groups, place_ref, *refs):
    xt_ref, updates, rest = refs[0], refs[1 : 1 + groups], refs[1 + groups :]
    forcing_ref, mask_ref, scale_ref, out_ref, piece_v, upd_v, forcing_v, out_v, sems = rest
    per = piece_v.shape[1]
    loads = []
    for d in range(groups):
        first = jnp.bitwise_xor(place_ref[0], d) * per
        loads.append(
            [
                pltpu.make_async_copy(
                    xt_ref.at[pl.ds(first, per)], piece_v.at[d], sems.at[0, d]
                ),
                pltpu.make_async_copy(updates[d], upd_v.at[d], sems.at[1, d]),
                pltpu.make_async_copy(
                    forcing_ref.at[pl.ds(first, per)], forcing_v.at[d], sems.at[2, d]
                ),
            ]
        )
        for load in loads[d]:
            load.start()
    scale = scale_ref[...]
    stores = []
    for d in range(groups):
        first = jnp.bitwise_xor(place_ref[0], d) * per
        for load in loads[d]:
            load.wait()
        for s in range(per):
            total = piece_v[d, s].astype(f32) + scale[None] * upd_v[d, s].astype(f32)
            total = total + forcing_v[d, s].astype(f32)
            total = mask_ref[first + s].astype(f32)[:, None, :] * total
            out_v[d, :, s] = jnp.swapaxes(total, 0, 1).astype(bf16)
        stores.append(
            pltpu.make_async_copy(out_v.at[d], out_ref.at[:, pl.ds(first, per)], sems.at[3, d])
        )
        stores[d].start()
    for store in stores:
        store.wait()


def final_step(place, xt, updates, forcing, cell_mask, layer_scale):
    slot_count, block_rows, chan_local, block_cols = forcing.shape
    groups = len(updates)
    per = slot_count // groups
    return pl.pallas_call(
        functools.partial(final_kernel, groups),
        out_shape=shape((chan_local, slot_count, block_rows, block_cols)),
        in_specs=[SMEM] + [ANY] * (groups + 2) + [VMEM, VMEM],
        out_specs=ANY,
        scratch_shapes=[pltpu.VMEM((groups,) + updates[0].shape, bf16)] * 3
        + [
            pltpu.VMEM((groups, chan_local, per, block_rows, block_cols), bf16),
            pltpu.SemaphoreType.DMA((4, groups)),
        ],
        compiler_params=params(),
        name="final_step",
    )(place, xt, *updates, forcing, cell_mask, layer_scale.astype(f32)[:, None])


def on_device(
    ocean_state,
    atmos,
    flux_weight,
    conv_weight,
    conv_bias,
    norm_gain,
    in_weight,
    in_bias,
    out_weight,
    layer_scale,
    cell_mask,
    neighbours,
    remap,
):
    chan_local, slot_count, block_rows, block_cols = ocean_state.shape
    groups = lax.axis_size(GROUP)
    tile_count = lax.axis_size("tile")
    hid_local = in_weight.shape[1]
    place = jnp.stack([lax.axis_index(GROUP), lax.axis_index("ens")])
    first_slot = (lax.axis_index("tile") - 1) * slot_count

    xt, strips, packed, part = start_step(
        place, groups, ocean_state, conv_weight, conv_bias, norm_gain, in_weight, in_bias, out_weight
    )
    up = [(i, i + 1) for i in range(tile_count - 1)]
    strips_prev = lax.ppermute(strips, "tile", up)
    strips_next = lax.ppermute(strips, "tile", [(b, a) for a, b in up])
    parts, starts = exchange_weights(packed, part)
    bodies = lax.all_to_all(
        xt.reshape((groups, slot_count // groups) + xt.shape[1:]), GROUP, 0, 0, tiled=True
    )
    entries, at = rim_places(neighbours, first_slot, block_rows)
    chosen = onehot_of(at, 3 * block_cols)
    flux = fluxes_of(atmos, flux_weight)
    strips_prev, strips_next, flux = lax.optimization_barrier((strips_prev, strips_next, flux))
    rims = rims_of(place, entries, chosen, strips_prev, strips, strips_next, groups)
    rims = trade(rims)
    table = gather_flux(flux)
    weights = unpack_weights(parts, starts, groups, chan_local, hid_local)
    updates = block_step(place, bodies, rims, weights)
    _, table = lax.optimization_barrier((updates[0], table))
    updates = trade(updates)
    forcing = forcing_of(table, remap, atmos.shape[0], chan_local)
    return final_step(place, xt, updates, forcing, cell_mask, layer_scale)


def solution(mesh):
    placed = (
        P(("chan", "sec"), ("ens", "tile"), None, None),
        P(("ens", "tile"), None),
        P(None, ("chan", "sec")),
        P(None, None, ("chan", "sec")),
        P(("chan", "sec")),
        P(("chan", "sec")),
        P(None, ("chan", "sec")),
        P(("chan", "sec")),
        P(("chan", "sec"), None),
        P(("chan", "sec")),
        P("tile", None, None),
        P("tile", None),
        P("tile", None, None),
    )
    return jax.shard_map(
        on_device,
        mesh=mesh,
        in_specs=placed,
        out_specs=P(("chan", "sec"), ("ens", "tile"), None, None),
        check_vma=False,
    )
```

profile of v0, /device:TPU:0, one launch (start us, length us, event | category | flops | bytes accessed | tf_op | source)
XLA Modules:
  0.0 75.4 jit_solution(18008236029619956330)
XLA Ops:
  0.0 0.6 pad_add_fusion.1.place_ref
  0.6 4.3 %start_step.1 = (bf16[16,4,64,128]{3,2,1,0:T(8,128)(2,1)}, bf16[33,64,128]{2,1,0:T(8,128)(2,1)}, bf16[1120,256]{1,0:T(8,128)(2,1)}, bf16[560,256]{1,0:T(8,128)(2,1)}) custom-call(s32[2]{0:T(128)} %pad_add_fusion.1.place_ref, bf16[64,16,4,128]{3,2,1,0:T(4,128)(2,1)} %state_ref.1, bf16[9,64,256]{2,1,0:T(8,128)(2,1)} %bitcast.26, bf16[1,64]{1,0:T(2,128)(2,1)} %bitcast.28, ...), custom_call_target="tpu_custom_call" | custom-call | tf_op jit(solution)/shard_map/start_step/pallas_call | solution.py:103
  4.9 5.7 %collective-permute-start = (bf16[33,64,128]{2,1,0:T(8,128)(2,1)}, bf16[33,64,128]{2,1,0:T(8,128)(2,1)}, u32[]{:S(2)}, u32[]{:S(2)}) collective-permute-start(bf16[33,64,128]{2,1,0:T(8,128)(2,1)} %get-tuple-element.32.own_ref), channel_id=1, source_target_pairs={{0,4},{4,8},{8,12},{1,5},{5,9},{9,13},{2,6},{6,10},{10,14},{3,7},{... | collective-permute-start | bytes 1622024 | tf_op jit(solution)/shard_map/ppermute | solution.py:577
  10.7 1.3 %collective-permute-start.1 = (bf16[33,64,128]{2,1,0:T(8,128)(2,1)}, bf16[33,64,128]{2,1,0:T(8,128)(2,1)}, u32[]{:S(2)}, u32[]{:S(2)}) collective-permute-start(bf16[33,64,128]{2,1,0:T(8,128)(2,1)} %get-tuple-element.32.own_ref), channel_id=1, source_target_pairs={{4,0},{8,4},{12,8},{5,1},{9,5},{13,9},{6,2},{10,6},{14,10},{7,3},{... | collective-permute-start | bytes 1622024 | tf_op jit(solution)/shard_map/ppermute | solution.py:578
  12.0 1.6 %collective-permute-start.5 = (bf16[560,256]{1,0:T(8,128)(2,1)}, bf16[560,256]{1,0:T(8,128)(2,1)S(1)}, u32[]{:S(2)}, u32[]{:S(2)}) collective-permute-start(bf16[560,256]{1,0:T(8,128)(2,1)} %get-tuple-element.40), channel_id=1, source_target_pairs={{0,2},{2,0},{1,3},{3,1},{4,6},{6,4},{5,7},{7,5},{8,10},{10,8},{9,1... | collective-permute-start | bytes 860168 | tf_op jit(solution)/shard_map/ppermute | solution.py:195
  13.5 3.6 %all-to-all-start = ((bf16[4,4,4,64,128]{4,3,2,1,0:T(8,128)(2,1)}), bf16[4,4,4,64,128]{4,3,2,1,0:T(8,128)(2,1)S(1)}, u32[]{:S(2)}, u32[]{:S(2)}) async-start(bf16[4,4,4,64,128]{4,3,2,1,0:T(8,128)(2,1)} %bitcast.24), calls=%async_computation | async-start | bytes 2097152 | tf_op jit(solution)/shard_map/all_to_all | solution.py:580
  17.3 3.6 %collective-permute-done.5.refs_2_ = bf16[560,256]{1,0:T(8,128)(2,1)S(1)} collective-permute-done((bf16[560,256]{1,0:T(8,128)(2,1)}, bf16[560,256]{1,0:T(8,128)(2,1)S(1)}, u32[]{:S(2)}, u32[]{:S(2)}) %collective-permute-start.5) | collective-permute-done | bytes 286752 | tf_op jit(solution)/shard_map/ppermute | solution.py:195
  20.9 1.5 %collective-permute-start.7 = (bf16[560,256]{1,0:T(8,128)(2,1)S(1)}, bf16[560,256]{1,0:T(8,128)(2,1)}, u32[]{:S(2)}, u32[]{:S(2)}) collective-permute-start(bf16[560,256]{1,0:T(8,128)(2,1)S(1)} %collective-permute-done.5.refs_2_), channel_id=1, source_target_pairs={{0,16},{16,0},{1,17},{17,1},{2,18},{18,2},{3,19},{19,3},{4,20},{20... | collective-permute-start | bytes 860168 | tf_op jit(solution)/shard_map/ppermute | solution.py:195
  22.4 0.0 collective-permute-start.6
  22.4 0.1 copy.14
  22.5 0.1 copy.15
  22.6 0.1 copy.16
  22.7 0.1 copy.17
  22.8 0.1 copy.18
  22.8 0.1 copy.19
  22.9 0.1 copy.20
  23.0 0.1 copy.21
  23.1 0.1 copy.22
  23.2 0.1 copy.23
  23.3 0.1 copy.24
  23.3 0.1 copy.25
  23.4 0.1 stack.52
  23.5 0.1 reshape.65.at_ref
  23.6 0.1 onehot.1.chosen_ref
  23.7 0.1 copy.26.refs_7_
  23.8 0.6 fluxes.1
  24.3 0.1 stack.59.starts_ref
  24.4 0.5 collective-permute-start.8
  24.9 3.2 %collective-permute-done.7.refs_3_ = bf16[560,256]{1,0:T(8,128)(2,1)} collective-permute-done((bf16[560,256]{1,0:T(8,128)(2,1)S(1)}, bf16[560,256]{1,0:T(8,128)(2,1)}, u32[]{:S(2)}, u32[]{:S(2)}) %collective-permute-start.7) | collective-permute-done | bytes 286752 | tf_op jit(solution)/shard_map/ppermute | solution.py:195
  28.2 0.0 collective-permute-done.1.next_ref
  28.2 1.0 %copy-done.2 = bf16[33,64,128]{2,1,0:T(8,128)(2,1)S(1)} copy-done((bf16[33,64,128]{2,1,0:T(8,128)(2,1)S(1)}, bf16[33,64,128]{2,1,0:T(8,128)(2,1)}, u32[]{:S(2)}) %copy-start.2) | copy-done | bytes 540696
  29.2 1.4 %rims.1 = (bf16[9,64,128]{2,1,0:T(8,128)(2,1)S(1)}, bf16[9,64,128]{2,1,0:T(8,128)(2,1)S(1)}, bf16[9,64,128]{2,1,0:T(8,128)(2,1)S(1)}, bf16[9,64,128]{2,1,0:T(8,128)(2,1)S(1)}) custom-call(s32[2]{0:T(128)S(1)} %copy-done.5, s32[2,16]{1,0:T(2,128)S(1)} %pad_add_fusion.entry_ref, bf16[384,256]{1,0:T(8,128)(2,1)S(1)} %onehot.1.chosen_ref, ...), custom_call_target="tpu_custom_call" | custom-call | tf_op jit(solution)/shard_map/rims/pallas_call | solution.py:306
  30.7 0.6 collective-permute-start.2
  31.2 1.9 %collective-permute-start.3 = (bf16[9,64,128]{2,1,0:T(8,128)(2,1)S(1)}, bf16[9,64,128]{2,1,0:T(8,128)(2,1)S(1)}, u32[]{:S(2)}, u32[]{:S(2)}) collective-permute-start(bf16[9,64,128]{2,1,0:T(8,128)(2,1)S(1)} %get-tuple-element.37), channel_id=1, source_target_pairs={{0,2},{1,3},{2,0},{3,1},{4,6},{5,7},{6,4},{7,5},{8,10},{9,11},{10,... | collective-permute-start | bytes 442376 | tf_op jit(solution)/shard_map/ppermute | solution.py:135
  33.1 0.1 add_select_fusion
  33.2 2.1 %collective-permute-start.13 = (bf16[1024,128]{1,0:T(8,128)(2,1)S(1)}, bf16[1024,128]{1,0:T(8,128)(2,1)}, u32[]{:S(2)}, u32[]{:S(2)}) collective-permute-start(bf16[1024,128]{1,0:T(8,128)(2,1)S(1)} %fluxes.1), channel_id=1, source_target_pairs={{0,4},{4,8},{8,12},{12,0},{1,5},{5,9},{9,13},{13,1},{2,6},{6,10},{... | collective-permute-start | bytes 786440 | tf_op jit(solution)/shard_map/ppermute | solution.py:462
  35.3 2.5 %collective-permute-start.14 = (bf16[1024,128]{1,0:T(8,128)(2,1)S(1)}, bf16[1024,128]{1,0:T(8,128)(2,1)}, u32[]{:S(2)}, u32[]{:S(2)}) collective-permute-start(bf16[1024,128]{1,0:T(8,128)(2,1)S(1)} %fluxes.1), channel_id=1, source_target_pairs={{0,8},{4,12},{8,0},{12,4},{1,9},{5,13},{9,1},{13,5},{2,10},{6,14},... | collective-permute-start | bytes 786440 | tf_op jit(solution)/shard_map/ppermute | solution.py:462
  37.8 1.8 %unpack_weights.1 = (bf16[256,2304]{1,0:T(8,128)(2,1)S(1)}, bf16[1024,256]{1,0:T(8,128)(2,1)S(1)}, bf16[256,1024]{1,0:T(8,128)(2,1)S(1)}, f32[256,32]{1,0:T(8,128)S(1)}, f32[1024,32]{1,0:T(8,128)S(1)}) custom-call(s32[6]{0:T(128)S(1)} %stack.59.starts_ref, bf16[1120,256]{1,0:T(8,128)(2,1)} %get-tuple-element.41.refs_0_, ...), custom_call_target="tpu_custom_call" | custom-call | tf_op jit(solution)/shard_map/unpack_weights/pallas_call | solution.py:177
  39.7 0.8 %copy-done.6 = bf16[1024,256]{1,0:T(8,128)(2,1)} copy-done((bf16[1024,256]{1,0:T(8,128)(2,1)}, bf16[1024,256]{1,0:T(8,128)(2,1)S(1)}, u32[]{:S(2)}) %copy-start.6) | copy-done | bytes 524312
  40.4 0.8 %copy-done.8 = bf16[256,1024]{1,0:T(8,128)(2,1)} copy-done((bf16[256,1024]{1,0:T(8,128)(2,1)}, bf16[256,1024]{1,0:T(8,128)(2,1)S(1)}, u32[]{:S(2)}) %copy-start.8) | copy-done | bytes 524312
  41.3 0.8 %copy-done.10 = f32[1024,32]{1,0:T(8,128)} copy-done((f32[1024,32]{1,0:T(8,128)}, f32[1024,32]{1,0:T(8,128)S(1)}, u32[]{:S(2)}) %copy-start.10) | copy-done | bytes 131096
  42.1 0.7 copy-done.16
  42.7 0.0 collective-permute-done.2.refs_2_
  42.7 0.6 collective-permute-start.15
  43.4 0.0 collective-permute-done.3.refs_3_
  43.4 0.7 copy-done.12
  44.0 0.0 collective-permute-done.4.refs_4_
  44.0 0.7 copy-done.14
  44.7 1.0 %copy-done.7 = bf16[1024,256]{1,0:T(8,128)(2,1)S(1)} copy-done((bf16[1024,256]{1,0:T(8,128)(2,1)S(1)}, bf16[1024,256]{1,0:T(8,128)(2,1)}, u32[]{:S(2)}) %copy-start.7) | copy-done | bytes 524312
  45.7 1.0 %copy-done.9 = bf16[256,1024]{1,0:T(8,128)(2,1)S(1)} copy-done((bf16[256,1024]{1,0:T(8,128)(2,1)S(1)}, bf16[256,1024]{1,0:T(8,128)(2,1)}, u32[]{:S(2)}) %copy-start.9) | copy-done | bytes 524312
  46.8 1.0 %copy-done.11 = f32[1024,32]{1,0:T(8,128)S(1)} copy-done((f32[1024,32]{1,0:T(8,128)S(1)}, f32[1024,32]{1,0:T(8,128)}, u32[]{:S(2)}) %copy-start.11) | copy-done | bytes 131096
  47.8 0.9 %copy-done.13 = bf16[9,64,128]{2,1,0:T(8,128)(2,1)S(1)} copy-done((bf16[9,64,128]{2,1,0:T(8,128)(2,1)S(1)}, bf16[9,64,128]{2,1,0:T(8,128)(2,1)}, u32[]{:S(2)}) %copy-start.13) | copy-done | bytes 147480
  48.7 0.9 %copy-done.15 = bf16[9,64,128]{2,1,0:T(8,128)(2,1)S(1)} copy-done((bf16[9,64,128]{2,1,0:T(8,128)(2,1)S(1)}, bf16[9,64,128]{2,1,0:T(8,128)(2,1)}, u32[]{:S(2)}) %copy-start.15) | copy-done | bytes 147480
  49.6 0.9 %copy-done.17 = f32[256,32]{1,0:T(8,128)S(1)} copy-done((f32[256,32]{1,0:T(8,128)S(1)}, f32[256,32]{1,0:T(8,128)}, u32[]{:S(2)}) %copy-start.17) | copy-done | bytes 32792
  50.5 7.9 %block_step.1 = (bf16[4,4,64,128]{3,2,1,0:T(8,128)(2,1)S(1)}, bf16[4,4,64,128]{3,2,1,0:T(8,128)(2,1)S(1)}, bf16[4,4,64,128]{3,2,1,0:T(8,128)(2,1)S(1)}, bf16[4,4,64,128]{3,2,1,0:T(8,128)(2,1)S(1)}) custom-call(s32[2]{0:T(128)S(1)} %copy-done.5, bf16[4,4,4,64,128]{4,3,2,1,0:T(8,128)(2,1)S(1)} %all-to-all-done.refs_0_, ...), custom_call_target="tpu_custom_call" | custom-call | flops 4563402752 | bytes 8388608 | tf_op jit(solution)/shard_map/block_step/pallas_call | solution.py:395
  58.5 0.1 collective-permute-start.10
  58.6 1.5 %collective-permute-start.11 = (bf16[4,4,64,128]{3,2,1,0:T(8,128)(2,1)S(1)}, bf16[4,4,64,128]{3,2,1,0:T(8,128)(2,1)S(1)}, u32[]{:S(2)}, u32[]{:S(2)}) collective-permute-start(bf16[4,4,64,128]{3,2,1,0:T(8,128)(2,1)S(1)} %get-tuple-element.50), channel_id=1, source_target_pairs={{0,2},{1,3},{2,0},{3,1},{4,6},{5,7},{6,4},{7,5},{8,10},{9,11},{10,... | collective-permute-start | bytes 786440 | tf_op jit(solution)/shard_map/ppermute | solution.py:135
  60.1 0.4 collective-permute-start.12
  60.5 1.2 %maximum_convert_fusion = f32[4096,128]{1,0:T(8,128)S(1)} fusion(bf16[1024,128]{1,0:T(8,128)(2,1)} %collective-permute-done.15, bf16[1024,128]{1,0:T(8,128)(2,1)} %collective-permute-done.14, bf16[1024,128]{1,0:T(8,128)(2,1)} %collective-permute-done.13, bf16[1024,128]{1,0:T(8,128)(2,1)S(1)} %fluxes.1), kind=kLoop, calls=%fused_computation | loop fusion | flops 4194304 | bytes 3145728 | tf_op jit(solution)/shard_map/convert_element_type | solution.py:478
  61.7 0.0 copy-start
  61.7 0.0 copy-start.4
  61.7 9.7 %forcing.1.refs_5_ = bf16[16,4,64,128]{3,2,1,0:T(8,128)(2,1)S(1)} custom-call(s32[64,128]{1,0:T(8,128)S(1)} %get-tuple-element.58.row_ref, s32[64,128]{1,0:T(8,128)S(1)} %get-tuple-element.57.side_ref, f32[4096,1,128]{2,1,0:T(1,128)S(1)} %bitcast.23), custom_call_target="tpu_custom_call" | custom-call | bytes 33554432 | tf_op jit(solution)/shard_map/forcing/pallas_call | solution.py:479
  71.5 1.0 %collective-permute-done.12.refs_4_ = bf16[4,4,64,128]{3,2,1,0:T(8,128)(2,1)S(1)} collective-permute-done((bf16[4,4,64,128]{3,2,1,0:T(8,128)(2,1)S(1)}, bf16[4,4,64,128]{3,2,1,0:T(8,128)(2,1)S(1)}, u32[]{:S(2)}, u32[]{:S(2)}) %collective-permute-start.12) | collective-permute-done | bytes 262176 | tf_op jit(solution)/shard_map/ppermute | solution.py:135
  72.5 2.7 %final_step.1 = bf16[64,16,4,128]{3,2,1,0:T(4,128)(2,1)} custom-call(s32[2]{0:T(128)S(1)} %copy-done.5, bf16[16,4,64,128]{3,2,1,0:T(8,128)(2,1)S(1)} %copy-done, bf16[4,4,64,128]{3,2,1,0:T(8,128)(2,1)S(1)} %get-tuple-element.48.refs_1_, bf16[4,4,64,128]{3,2,1,0:T(8,128)(2,1)S(1)} %collective-permute-done.10.refs_2_, ...), custom_call_target="tpu_custom_call" | custom-call | tf_op jit(solution)/shard_map/final_step/pallas_call | solution.py:536
  (46 shorter events, 0.1 us)
Async XLA Ops:
  0.0 17.2 %copy-start.19 = (s32[16,8]{0,1:T(8,128)S(1)}, s32[16,8]{0,1:T(8,128)}, u32[]{:S(2)}) copy-start(s32[16,8]{0,1:T(8,128)} %param.24) | copy-start | bytes 1540
  0.0 22.4 %copy-start.20 = (bf16[64]{0:T(256)(128)(2,1)S(1)}, bf16[64]{0:T(256)(128)(2,1)}, u32[]{:S(2)}) copy-start(bf16[64]{0:T(256)(128)(2,1)} %param.22) | copy-start | bytes 388
  0.6 23.2 %copy-start.1 = (bf16[2048,384]{1,0:T(8,128)(2,1)S(1)}, bf16[2048,384]{1,0:T(8,128)(2,1)}, u32[]{:S(2)}) copy-start(bf16[2048,384]{1,0:T(8,128)(2,1)} %atmos_ref.1) | copy-start | bytes 4718596
  0.6 23.2 %copy-start.3 = (bf16[384,64]{0,1:T(8,128)(2,1)S(1)}, bf16[384,64]{0,1:T(8,128)(2,1)}, u32[]{:S(2)}) copy-start(bf16[384,64]{0,1:T(8,128)(2,1)} %param.15) | copy-start | bytes 147460
  4.9 23.2 %collective-permute-start = (bf16[33,64,128]{2,1,0:T(8,128)(2,1)}, bf16[33,64,128]{2,1,0:T(8,128)(2,1)}, u32[]{:S(2)}, u32[]{:S(2)}) collective-permute-start(bf16[33,64,128]{2,1,0:T(8,128)(2,1)} %get-tuple-element.32.own_ref), channel_id=1, source_target_pairs={{0,4},{4,8},{8,12},{1,5},{5,9},{9,13},{2,6},{6,10},{10,14},{3,7},{... | collective-permute-start | bytes 1622024 | tf_op jit(solution)/shard_map/ppermute | solution.py:577
  10.7 17.5 %collective-permute-start.1 = (bf16[33,64,128]{2,1,0:T(8,128)(2,1)}, bf16[33,64,128]{2,1,0:T(8,128)(2,1)}, u32[]{:S(2)}, u32[]{:S(2)}) collective-permute-start(bf16[33,64,128]{2,1,0:T(8,128)(2,1)} %get-tuple-element.32.own_ref), channel_id=1, source_target_pairs={{4,0},{8,4},{12,8},{5,1},{9,5},{13,9},{6,2},{10,6},{14,10},{7,3},{... | collective-permute-start | bytes 1622024 | tf_op jit(solution)/shard_map/ppermute | solution.py:578
  12.0 8.9 %collective-permute-start.5 = (bf16[560,256]{1,0:T(8,128)(2,1)}, bf16[560,256]{1,0:T(8,128)(2,1)S(1)}, u32[]{:S(2)}, u32[]{:S(2)}) collective-permute-start(bf16[560,256]{1,0:T(8,128)(2,1)} %get-tuple-element.40), channel_id=1, source_target_pairs={{0,2},{2,0},{1,3},{3,1},{4,6},{6,4},{5,7},{7,5},{8,10},{10,8},{9,1... | collective-permute-start | bytes 860168 | tf_op jit(solution)/shard_map/ppermute | solution.py:195
  13.5 11.4 %copy-start.18 = (s32[16,4,128]{2,1,0:T(4,128)S(1)}, s32[16,4,128]{2,1,0:T(4,128)}, u32[]{:S(2)}) copy-start(s32[16,4,128]{2,1,0:T(4,128)} %param.25) | copy-start | bytes 98308
  13.5 14.6 %copy-start.5 = (s32[2]{0:T(128)S(1)}, s32[2]{0:T(128)}, u32[]{:S(2)}) copy-start(s32[2]{0:T(128)} %pad_add_fusion.1.place_ref) | copy-start | bytes 28
  13.5 31.2 %all-to-all-start = ((bf16[4,4,4,64,128]{4,3,2,1,0:T(8,128)(2,1)}), bf16[4,4,4,64,128]{4,3,2,1,0:T(8,128)(2,1)S(1)}, u32[]{:S(2)}, u32[]{:S(2)}) async-start(bf16[4,4,4,64,128]{4,3,2,1,0:T(8,128)(2,1)} %bitcast.24), calls=%async_computation | async-start | bytes 2097152 | tf_op jit(solution)/shard_map/all_to_all | solution.py:580
  20.9 7.3 %collective-permute-start.7 = (bf16[560,256]{1,0:T(8,128)(2,1)S(1)}, bf16[560,256]{1,0:T(8,128)(2,1)}, u32[]{:S(2)}, u32[]{:S(2)}) collective-permute-start(bf16[560,256]{1,0:T(8,128)(2,1)S(1)} %collective-permute-done.5.refs_2_), channel_id=1, source_target_pairs={{0,16},{16,0},{1,17},{17,1},{2,18},{18,2},{3,19},{19,3},{4,20},{20... | collective-permute-start | bytes 860168 | tf_op jit(solution)/shard_map/ppermute | solution.py:195
  22.4 12.9 %collective-permute-start.6 = (bf16[1120,256]{1,0:T(8,128)(2,1)}, bf16[1120,256]{1,0:T(8,128)(2,1)}, u32[]{:S(2)}, u32[]{:S(2)}) collective-permute-start(bf16[1120,256]{1,0:T(8,128)(2,1)} %get-tuple-element.41.refs_0_), channel_id=1, source_target_pairs={{0,1},{1,0},{2,3},{3,2},{4,5},{5,4},{6,7},{7,6},{8,9},{9,8},{10,11... | collective-permute-start | bytes 1720328 | tf_op jit(solution)/shard_map/ppermute | solution.py:195
  24.4 8.7 %collective-permute-start.8 = (bf16[560,256]{1,0:T(8,128)(2,1)S(1)}, bf16[560,256]{1,0:T(8,128)(2,1)S(1)}, u32[]{:S(2)}, u32[]{:S(2)}) collective-permute-start(bf16[560,256]{1,0:T(8,128)(2,1)S(1)} %collective-permute-done.5.refs_2_), channel_id=1, source_target_pairs={{0,1},{1,0},{2,3},{3,2},{4,5},{5,4},{6,7},{7,6},{8,9},{9,8},{10,11... | collective-permute-start | bytes 860168 | tf_op jit(solution)/shard_map/ppermute | solution.py:195
  28.1 5.0 %collective-permute-start.9 = (bf16[560,256]{1,0:T(8,128)(2,1)}, bf16[560,256]{1,0:T(8,128)(2,1)S(1)}, u32[]{:S(2)}, u32[]{:S(2)}) collective-permute-start(bf16[560,256]{1,0:T(8,128)(2,1)} %collective-permute-done.7.refs_3_), channel_id=1, source_target_pairs={{0,1},{1,0},{2,3},{3,2},{4,5},{5,4},{6,7},{7,6},{8,9},{9,8},{10,11... | collective-permute-start | bytes 860168 | tf_op jit(solution)/shard_map/ppermute | solution.py:195
  28.2 1.0 %copy-start.2 = (bf16[33,64,128]{2,1,0:T(8,128)(2,1)S(1)}, bf16[33,64,128]{2,1,0:T(8,128)(2,1)}, u32[]{:S(2)}) copy-start(bf16[33,64,128]{2,1,0:T(8,128)(2,1)} %get-tuple-element.32.own_ref) | copy-start | bytes 1622020
  30.7 12.1 %collective-permute-start.2 = (bf16[9,64,128]{2,1,0:T(8,128)(2,1)S(1)}, bf16[9,64,128]{2,1,0:T(8,128)(2,1)S(1)}, u32[]{:S(2)}, u32[]{:S(2)}) collective-permute-start(bf16[9,64,128]{2,1,0:T(8,128)(2,1)S(1)} %get-tuple-element.36), channel_id=1, source_target_pairs={{0,1},{1,0},{2,3},{3,2},{4,5},{5,4},{6,7},{7,6},{8,9},{9,8},{10,11... | collective-permute-start | bytes 442376 | tf_op jit(solution)/shard_map/ppermute | solution.py:135
  31.2 12.1 %collective-permute-start.3 = (bf16[9,64,128]{2,1,0:T(8,128)(2,1)S(1)}, bf16[9,64,128]{2,1,0:T(8,128)(2,1)S(1)}, u32[]{:S(2)}, u32[]{:S(2)}) collective-permute-start(bf16[9,64,128]{2,1,0:T(8,128)(2,1)S(1)} %get-tuple-element.37), channel_id=1, source_target_pairs={{0,2},{1,3},{2,0},{3,1},{4,6},{5,7},{6,4},{7,5},{8,10},{9,11},{10,... | collective-permute-start | bytes 442376 | tf_op jit(solution)/shard_map/ppermute | solution.py:135
  33.1 10.9 %collective-permute-start.4 = (bf16[9,64,128]{2,1,0:T(8,128)(2,1)S(1)}, bf16[9,64,128]{2,1,0:T(8,128)(2,1)S(1)}, u32[]{:S(2)}, u32[]{:S(2)}) collective-permute-start(bf16[9,64,128]{2,1,0:T(8,128)(2,1)S(1)} %get-tuple-element.38), channel_id=1, source_target_pairs={{0,3},{1,2},{2,1},{3,0},{4,7},{5,6},{6,5},{7,4},{8,11},{9,10},{10,... | collective-permute-start | bytes 442376 | tf_op jit(solution)/shard_map/ppermute | solution.py:135
  33.2 25.3 %collective-permute-start.13 = (bf16[1024,128]{1,0:T(8,128)(2,1)S(1)}, bf16[1024,128]{1,0:T(8,128)(2,1)}, u32[]{:S(2)}, u32[]{:S(2)}) collective-permute-start(bf16[1024,128]{1,0:T(8,128)(2,1)S(1)} %fluxes.1), channel_id=1, source_target_pairs={{0,4},{4,8},{8,12},{12,0},{1,5},{5,9},{9,13},{13,1},{2,6},{6,10},{... | collective-permute-start | bytes 786440 | tf_op jit(solution)/shard_map/ppermute | solution.py:462
  35.3 23.2 %collective-permute-start.14 = (bf16[1024,128]{1,0:T(8,128)(2,1)S(1)}, bf16[1024,128]{1,0:T(8,128)(2,1)}, u32[]{:S(2)}, u32[]{:S(2)}) collective-permute-start(bf16[1024,128]{1,0:T(8,128)(2,1)S(1)} %fluxes.1), channel_id=1, source_target_pairs={{0,8},{4,12},{8,0},{12,4},{1,9},{5,13},{9,1},{13,5},{2,10},{6,14},... | collective-permute-start | bytes 786440 | tf_op jit(solution)/shard_map/ppermute | solution.py:462
  39.7 0.8 %copy-start.6 = (bf16[1024,256]{1,0:T(8,128)(2,1)}, bf16[1024,256]{1,0:T(8,128)(2,1)S(1)}, u32[]{:S(2)}) copy-start(bf16[1024,256]{1,0:T(8,128)(2,1)S(1)} %get-tuple-element.44.refs_6_) | copy-start | bytes 1572868
  40.4 0.8 %copy-start.8 = (bf16[256,1024]{1,0:T(8,128)(2,1)}, bf16[256,1024]{1,0:T(8,128)(2,1)S(1)}, u32[]{:S(2)}) copy-start(bf16[256,1024]{1,0:T(8,128)(2,1)S(1)} %get-tuple-element.45.refs_7_) | copy-start | bytes 1572868
  41.3 0.8 %copy-start.10 = (f32[1024,32]{1,0:T(8,128)}, f32[1024,32]{1,0:T(8,128)S(1)}, u32[]{:S(2)}) copy-start(f32[1024,32]{1,0:T(8,128)S(1)} %get-tuple-element.47.refs_9_) | copy-start | bytes 393220
  42.1 0.7 copy-start.16
  42.7 15.8 %collective-permute-start.15 = (bf16[1024,128]{1,0:T(8,128)(2,1)S(1)}, bf16[1024,128]{1,0:T(8,128)(2,1)}, u32[]{:S(2)}, u32[]{:S(2)}) collective-permute-start(bf16[1024,128]{1,0:T(8,128)(2,1)S(1)} %fluxes.1), channel_id=1, source_target_pairs={{0,12},{4,0},{8,4},{12,8},{1,13},{5,1},{9,5},{13,9},{2,14},{6,2},{... | collective-permute-start | bytes 786440 | tf_op jit(solution)/shard_map/ppermute | solution.py:462
  43.4 0.7 copy-start.12
  44.0 0.7 copy-start.14
  44.7 1.0 %copy-start.7 = (bf16[1024,256]{1,0:T(8,128)(2,1)S(1)}, bf16[1024,256]{1,0:T(8,128)(2,1)}, u32[]{:S(2)}) copy-start(bf16[1024,256]{1,0:T(8,128)(2,1)} %copy-done.6) | copy-start | bytes 1572868
  45.7 1.0 %copy-start.9 = (bf16[256,1024]{1,0:T(8,128)(2,1)S(1)}, bf16[256,1024]{1,0:T(8,128)(2,1)}, u32[]{:S(2)}) copy-start(bf16[256,1024]{1,0:T(8,128)(2,1)} %copy-done.8) | copy-start | bytes 1572868
  46.8 1.0 %copy-start.11 = (f32[1024,32]{1,0:T(8,128)S(1)}, f32[1024,32]{1,0:T(8,128)}, u32[]{:S(2)}) copy-start(f32[1024,32]{1,0:T(8,128)} %copy-done.10) | copy-start | bytes 393220
  47.8 0.9 %copy-start.13 = (bf16[9,64,128]{2,1,0:T(8,128)(2,1)S(1)}, bf16[9,64,128]{2,1,0:T(8,128)(2,1)}, u32[]{:S(2)}) copy-start(bf16[9,64,128]{2,1,0:T(8,128)(2,1)} %copy-done.12) | copy-start | bytes 442372
  48.7 0.9 %copy-start.15 = (bf16[9,64,128]{2,1,0:T(8,128)(2,1)S(1)}, bf16[9,64,128]{2,1,0:T(8,128)(2,1)}, u32[]{:S(2)}) copy-start(bf16[9,64,128]{2,1,0:T(8,128)(2,1)} %copy-done.14) | copy-start | bytes 442372
  49.6 0.9 %copy-start.17 = (f32[256,32]{1,0:T(8,128)S(1)}, f32[256,32]{1,0:T(8,128)}, u32[]{:S(2)}) copy-start(f32[256,32]{1,0:T(8,128)} %copy-done.16) | copy-start | bytes 98308
  58.5 12.9 %collective-permute-start.10 = (bf16[4,4,64,128]{3,2,1,0:T(8,128)(2,1)S(1)}, bf16[4,4,64,128]{3,2,1,0:T(8,128)(2,1)S(1)}, u32[]{:S(2)}, u32[]{:S(2)}) collective-permute-start(bf16[4,4,64,128]{3,2,1,0:T(8,128)(2,1)S(1)} %get-tuple-element.49), channel_id=1, source_target_pairs={{0,1},{1,0},{2,3},{3,2},{4,5},{5,4},{6,7},{7,6},{8,9},{9,8},{10,11... | collective-permute-start | bytes 786440 | tf_op jit(solution)/shard_map/ppermute | solution.py:135
  58.6 12.9 %collective-permute-start.11 = (bf16[4,4,64,128]{3,2,1,0:T(8,128)(2,1)S(1)}, bf16[4,4,64,128]{3,2,1,0:T(8,128)(2,1)S(1)}, u32[]{:S(2)}, u32[]{:S(2)}) collective-permute-start(bf16[4,4,64,128]{3,2,1,0:T(8,128)(2,1)S(1)} %get-tuple-element.50), channel_id=1, source_target_pairs={{0,2},{1,3},{2,0},{3,1},{4,6},{5,7},{6,4},{7,5},{8,10},{9,11},{10,... | collective-permute-start | bytes 786440 | tf_op jit(solution)/shard_map/ppermute | solution.py:135
  60.1 12.4 %collective-permute-start.12 = (bf16[4,4,64,128]{3,2,1,0:T(8,128)(2,1)S(1)}, bf16[4,4,64,128]{3,2,1,0:T(8,128)(2,1)S(1)}, u32[]{:S(2)}, u32[]{:S(2)}) collective-permute-start(bf16[4,4,64,128]{3,2,1,0:T(8,128)(2,1)S(1)} %get-tuple-element.51), channel_id=1, source_target_pairs={{0,3},{1,2},{2,1},{3,0},{4,7},{5,6},{6,5},{7,4},{8,11},{9,10},{10,... | collective-permute-start | bytes 786440 | tf_op jit(solution)/shard_map/ppermute | solution.py:135
  61.7 10.8 %copy-start = (bf16[16,4,64,128]{3,2,1,0:T(8,128)(2,1)S(1)}, bf16[16,4,64,128]{3,2,1,0:T(8,128)(2,1)}, u32[]{:S(2)}) copy-start(bf16[16,4,64,128]{3,2,1,0:T(8,128)(2,1)} %get-tuple-element.31.refs_0_) | copy-start | bytes 3145732
  61.7 10.8 %copy-start.4 = (s32[16,4,128]{2,1,0:T(4,128)S(1)}, s32[16,4,128]{2,1,0:T(4,128)}, u32[]{:S(2)}) copy-start(s32[16,4,128]{2,1,0:T(4,128)} %refs_6_.1) | copy-start | bytes 98308
where the time goes:
time: 76.7 us; the launch traced here: 75.4 us
  Pallas kernels  28.5 us (37%)
  starting transfers between devices  23.9 us (31%)
  local copies, waits for them, and re-layouts  12.7 us (17%)
  waiting for transfers between devices  7.86 us (10%)
  other arithmetic  1.95 us (3%)
    unnamed x42, local copies, waits for them, and re-layouts  11.3 us
    pallas_call x1, Pallas kernels, forcing_of(): pl.pallas_call(forcing_kernel, out_shape=shape((slot_count, block_rows, c...  9.7 us
    pallas_call x1, Pallas kernels, block_step(): pl.pallas_call(functools.partial(block_kernel, groups), out_shape=(shape(...  7.93 us
    ppermute x5, waiting for transfers between devices, swap(): return lax.ppermute(value, axis, [(0, 1), (1, 0)])  6.82 us
    ppermute x1, starting transfers between devices, on_device(): strips_prev = lax.ppermute(strips, 'tile', up)  5.73 us
    ppermute x3, starting transfers between devices, gather_flux(): pieces.append(lax.ppermute(flux, 'tile', turn))  5.3 us
    ppermute x6, starting transfers between devices, send(): return lax.ppermute(piece, GROUP, [(i, i ^ d) for i in range(count)])  4.36 us
    pallas_call x1, Pallas kernels, start_step(): pl.pallas_call(start_kernel, out_shape=(shape((slot_count, block_rows, ch...  4.34 us
  transfers between devices with their start and end apart: 17, of which 3 were waited for; matrix products, arithmetic and copies ran while one was open for 4% of the time, Pallas kernels for 28%

commit v1 on v0

--- a/solution.py
+++ b/solution.py
@@ -29,28 +29,53 @@
     return lax.dot_general(a, b, (dims, ((), ())), preferred_element_type=f32)
 
 
-def start_kernel(
-    place_ref, state_ref, conv_ref, bias_ref, gain_ref, in_ref, in_bias_ref, out_ref, *refs
-):
-    xt_ref, strips_ref, pack_ref, part_ref, state_v, conv_v, in_v, out_v, sems = refs
-    groups, chan_local, per, block_rows, block_cols = state_v.shape
+def start_kernel(chips, *refs):
+    state_ref, conv_ref, bias_ref, gain_ref, in_ref, in_bias_ref, out_ref = refs[:7]
+    halves, strips_ref, pack_ref, part_ref = refs[7 : 7 + chips], *refs[7 + chips : 10 + chips]
+    state_v, conv_v, in_v, out_v, half_v, strips_v, pack_v, sems = refs[10 + chips :]
+    _, chan_local, span, block_rows, block_cols = state_v.shape
     taps, _, channels = conv_v.shape
     hid_local = out_v.shape[0]
+    chan = lax.axis_index("chan")
+    firsts = [jnp.bitwise_xor(chan, c) * span for c in range(chips)]
+    loads = [
+        pltpu.make_async_copy(
+            state_ref.at[:, pl.ds(firsts[c], span)], state_v.at[c], sems.at[c]
+        )
+        for c in range(chips)
+    ]
     copies = [
-        pltpu.make_async_copy(conv_ref, conv_v, sems.at[groups]),
-        pltpu.make_async_copy(in_ref, in_v, sems.at[groups + 1]),
-        pltpu.make_async_copy(out_ref, out_v, sems.at[groups + 2]),
+        pltpu.make_async_copy(conv_ref, conv_v, sems.at[chips]),
+        pltpu.make_async_copy(in_ref, in_v, sems.at[chips + 1]),
+        pltpu.make_async_copy(out_ref, out_v, sems.at[chips + 2]),
     ]
-    for copy in copies:
+    for copy in loads + copies:
         copy.start()
-    loads = []
-    for d in range(groups):
-        loads.append(
-            pltpu.make_async_copy(
-                state_ref.at[:, pl.ds(d * per, per)], state_v.at[d], sems.at[d]
-            )
-        )
-        loads[d].start()
+    stores = []
+
+    def store(source, target):
+        stores.append(pltpu.make_async_copy(source, target, sems.at[chips + 3 + len(stores)]))
+        stores[-1].start()
+
+    lane = lax.broadcasted_iota(jnp.int32, (chan_local, block_cols), 1)
+    ends = jnp.zeros((chan_local, block_cols), f32)
+    for c in range(chips):
+        loads[c].wait()
+        cols = jnp.zeros((chan_local, block_cols), f32)
+        for k in range(span):
+            rows = jnp.swapaxes(state_v[c, :, k].astype(f32), 0, 1)
+            packed = rows.astype(bf16)
+            half_v[c, k] = packed
+            strips_v[2 * (firsts[c] + k)] = packed[0]
+            strips_v[2 * (firsts[c] + k) + 1] = packed[block_rows - 1]
+            for r in range(block_rows):
+                spot = 2 * (block_rows * k + r)
+                turned = pltpu.roll(rows[r], spot + 1, 1)
+                cols = jnp.where((lane == spot) | (lane == spot + 1), turned, cols)
+        ends = ends + pltpu.roll(cols, firsts[c] * (2 * block_rows), 1)
+        store(half_v.at[c], halves[c])
+    strips_v[strips_v.shape[0] - 1] = ends.astype(bf16)
+    store(strips_v, strips_ref)
 
     def widen(ref):
         rows = ref[...].astype(f32)
@@ -64,63 +89,48 @@
         [widen(bias_ref), widen(gain_ref), widen(in_bias_ref), rest], axis=0
     )
     at = taps * chan_local
-    pack_ref[pl.ds(at + 2 * hid_local, BIAS_ROWS), :] = biases.astype(bf16)
     for copy in copies:
         copy.wait()
     for t in range(taps):
-        pack_ref[pl.ds(t * chan_local, chan_local), :] = conv_v[t]
-    pack_ref[pl.ds(at, hid_local), :] = in_v[...].astype(f32).T.astype(bf16)
-    pack_ref[pl.ds(at + hid_local, hid_local), :] = out_v[...]
+        pack_v[pl.ds(t * chan_local, chan_local), :] = conv_v[t]
+    pack_v[pl.ds(at, hid_local), :] = in_v[...].astype(f32).T.astype(bf16)
+    pack_v[pl.ds(at + hid_local, hid_local), :] = out_v[...]
+    pack_v[pl.ds(at + 2 * hid_local, BIAS_ROWS), :] = biases.astype(bf16)
     part = part_ref.shape[0]
-    part_ref[...] = pack_ref[pl.ds(pl.multiple_of(place_ref[1] * part, 16), part), :]
-
-    lane = lax.broadcasted_iota(jnp.int32, (chan_local, block_cols), 1)
-    cols = jnp.zeros((chan_local, block_cols), f32)
-    for d in range(groups):
-        loads[d].wait()
-        for s in range(per):
-            slot = d * per + s
-            rows = jnp.swapaxes(state_v[d, :, s].astype(f32), 0, 1)
-            packed = rows.astype(bf16)
-            xt_ref[slot] = packed
-            strips_ref[2 * slot] = packed[0]
-            strips_ref[2 * slot + 1] = packed[block_rows - 1]
-            for r in range(block_rows):
-                spot = 2 * (block_rows * slot + r)
-                turned = pltpu.roll(rows[r], spot + 1, 1)
-                cols = jnp.where((lane == spot) | (lane == spot + 1), turned, cols)
-    strips_ref[strips_ref.shape[0] - 1] = cols.astype(bf16)
-
-
-def start_step(
-    place, groups, state, conv_weight, conv_bias, norm_gain, in_weight, in_bias, out_weight
-):
+    store(pack_v, pack_ref)
+    store(pack_v.at[pl.ds(pl.multiple_of(lax.axis_index("ens") * part, 16), part)], part_ref)
+    for copy in stores:
+        copy.wait()
+
+
+def start_step(state, conv_weight, conv_bias, norm_gain, in_weight, in_bias, out_weight):
     chan_local, slot_count, block_rows, block_cols = state.shape
-    per = slot_count // groups
+    chips = lax.axis_size("chan")
+    span = slot_count // chips
     taps, channels, _ = conv_weight.shape
     hid_local = out_weight.shape[0]
     rows = taps * chan_local + 2 * hid_local + BIAS_ROWS
-    return pl.pallas_call(
-        start_kernel,
-        out_shape=(
-            shape((slot_count, block_rows, chan_local, block_cols)),
-            shape((2 * slot_count + 1, chan_local, block_cols)),
-            shape((rows, channels)),
-            shape((rows // 2, channels)),
-        ),
-        in_specs=[SMEM, ANY, ANY, VMEM, VMEM, ANY, VMEM, ANY],
-        out_specs=(VMEM,) * 4,
+    half = (span, block_rows, chan_local, block_cols)
+    strips = (2 * slot_count + 1, chan_local, block_cols)
+    *halves, strips, packed, part = pl.pallas_call(
+        functools.partial(start_kernel, chips),
+        out_shape=(shape(half),) * chips
+        + (shape(strips), shape((rows, channels)), shape((rows // 2, channels))),
+        in_specs=[ANY, ANY, VMEM, VMEM, ANY, VMEM, ANY],
+        out_specs=(ANY,) * (chips + 3),
         scratch_shapes=[
-            pltpu.VMEM((groups, chan_local, per, block_rows, block_cols), bf16),
+            pltpu.VMEM((chips, chan_local, span, block_rows, block_cols), bf16),
             pltpu.VMEM((taps, chan_local, channels), bf16),
             pltpu.VMEM((channels, hid_local), bf16),
             pltpu.VMEM((hid_local, channels), bf16),
-            pltpu.SemaphoreType.DMA((groups + 3,)),
+            pltpu.VMEM((chips,) + half, bf16),
+            pltpu.VMEM(strips, bf16),
+            pltpu.VMEM((rows, channels), bf16),
+            pltpu.SemaphoreType.DMA((2 * chips + 6,)),
         ],
         compiler_params=params(60),
         name="start_step",
     )(
-        place,
         state,
         conv_weight.transpose(0, 2, 1),
         conv_bias.reshape(-1, min(128, chan_local)),
@@ -129,6 +139,7 @@
         in_bias.reshape(-1, min(128, hid_local)),
         out_weight,
     )
+    return halves, strips, packed, part
 
 
 def send(piece, d, count):
@@ -195,23 +206,27 @@
     return lax.ppermute(value, axis, [(0, 1), (1, 0)])
 
 
-def exchange_weights(packed, part):
-    if lax.axis_size("ens") != 2 or lax.axis_size("chan") != 2 or lax.axis_size("sec") != 2:
-        whole = lax.all_gather(packed, GROUP, axis=0, tiled=True)
-        return [whole], jnp.zeros((1,), jnp.int32)
-    ens, chan, sec = (lax.axis_index(name) for name in ("ens", "chan", "sec"))
+def exchange_start(packed, part):
     near = swap(part, "chan")
     near, held = lax.optimization_barrier((near, packed))
-    far = swap(near, "ens")
-    other = swap(held, "sec")
-    near_other = swap(near, "sec")
-    far_other = swap(far, "sec")
+    return near, swap(near, "ens"), swap(held, "sec"), swap(near, "sec")
+
+
+def weight_places():
+    ens, chan, sec = (lax.axis_index(name) for name in ("ens", "chan", "sec"))
     own = 2 * (2 * chan + sec)
     beside = 2 * (2 * chan + 1 - sec)
     across = 2 * (2 * (1 - chan) + sec)
     corner = 2 * (2 * (1 - chan) + 1 - sec)
-    starts = [own, beside, across + ens, across + 1 - ens, corner + ens, corner + 1 - ens]
-    return [packed, other, near, far, near_other, far_other], jnp.stack(starts)
+    return jnp.stack([own, beside, across + ens, across + 1 - ens, corner + ens, corner + 1 - ens])
+
+
+def spread(halves):
+    chips = len(halves)
+    got = list(halves)
+    for c in range(1, chips):
+        got[c] = lax.ppermute(halves[c], "chan", [(i, i ^ c) for i in range(chips)])
+    return [pair for half in got for pair in (half, swap(half, "sec"))]
 
 
 def flux_kernel(atmos_ref, weight_ref, out_ref):
@@ -318,11 +333,12 @@
 
 
 def block_kernel(groups, place_ref, *refs):
-    body_ref, refs = refs[0], refs[1:]
+    bodies, refs = refs[:groups], refs[groups:]
     rims, refs = refs[:groups], refs[groups:]
     conv_ref, in_ref, out_ref, col_ref, hid_col_ref = refs[:5]
     updates, scratch = refs[5 : 5 + groups], refs[5 + groups :]
-    _, per, block_rows, chan_local, block_cols = body_ref.shape
+    per = (rims[0].shape[0] - 1) // 2
+    _, block_rows, chan_local, block_cols = bodies[0].shape
     channels = groups * chan_local
     hidden = in_ref.shape[0]
     me = place_ref[0]
@@ -333,10 +349,12 @@
     rows = [
         pl.multiple_of(jnp.bitwise_xor(me, d) * chan_local, chan_local) for d in range(groups)
     ]
-    rim_v, side_v = scratch[6:]
+    rim_v, side_v, body_v = scratch[6:]
+    first = me % (bodies[0].shape[0] // per) * per
     for d in range(groups):
         source = jnp.bitwise_xor(me, d)
         rim_v[source] = rims[d][...]
+        body_v[source] = bodies[d][pl.ds(first, per)]
         side_v[source] = pltpu.roll(rims[d][2 * per].astype(f32), block_cols - base, 1)
     for s in range(per):
         taken, hid, upd_v = scratch[3 * (s % 2) : 3 * (s % 2) + 3]
@@ -347,7 +365,7 @@
                 elif p == block_rows + 1:
                     mid = rim_v[d, 2 * s + 1]
                 else:
-                    mid = body_ref[d, s, p - 1]
+                    mid = body_v[d, s, p - 1]
                 wide = mid.astype(f32)
                 spot = 16 * s + p
                 left = jnp.where(
@@ -388,14 +406,17 @@
 
 
 def block_step(place, bodies, rims, weights):
-    groups, per, block_rows, chan_local, block_cols = bodies.shape
+    groups = len(bodies)
+    per = (rims[0].shape[0] - 1) // 2
+    _, block_rows, chan_local, block_cols = bodies[0].shape
+    piece = (per, block_rows, chan_local, block_cols)
     channels = groups * chan_local
     hidden = weights[1].shape[0]
     cells = per * block_rows * block_cols
     return pl.pallas_call(
         functools.partial(block_kernel, groups),
-        out_shape=(shape(bodies.shape[1:]),) * groups,
-        in_specs=[SMEM] + [VMEM] * (groups + 6),
+        out_shape=(shape(piece),) * groups,
+        in_specs=[SMEM] + [VMEM] * (2 * groups + 5),
         out_specs=(VMEM,) * groups,
         scratch_shapes=[
             pltpu.VMEM((9, channels, block_rows * block_cols), bf16),
@@ -406,6 +427,7 @@
         + [
             pltpu.VMEM((groups,) + rims[0].shape, bf16),
             pltpu.VMEM((groups, chan_local, block_cols), f32),
+            pltpu.VMEM((groups,) + piece, bf16),
         ],
         compiler_params=params(24),
         cost_estimate=pl.CostEstimate(
@@ -414,7 +436,7 @@
             transcendentals=0,
         ),
         name="block_step",
-    )(place, bodies, *rims, *weights)
+    )(place, *bodies, *rims, *weights)
 
 
 def forcing_kernel(row_ref, side_ref, wide, out_ref, even, odd):
@@ -490,21 +512,26 @@
     )(row, side, table)
 
 
-def final_kernel(groups, place_ref, *refs):
-    xt_ref, updates, rest = refs[0], refs[1 : 1 + groups], refs[1 + groups :]
-    forcing_ref, mask_ref, scale_ref, out_ref, piece_v, upd_v, forcing_v, out_v, sems = rest
+def final_kernel(chips, groups, place_ref, *refs):
+    halves, updates = refs[:chips], refs[chips : chips + groups]
+    forcing_ref, mask_ref, scale_ref, out_ref, piece_v, upd_v, forcing_v, out_v, sems = refs[
+        chips + groups :
+    ]
     per = piece_v.shape[1]
+    cores = groups // chips
     loads = []
     for d in range(groups):
-        first = jnp.bitwise_xor(place_ref[0], d) * per
+        group = jnp.bitwise_xor(place_ref[0], d)
         loads.append(
             [
                 pltpu.make_async_copy(
-                    xt_ref.at[pl.ds(first, per)], piece_v.at[d], sems.at[0, d]
+                    halves[d // cores].at[pl.ds(group % cores * per, per)],
+                    piece_v.at[d],
+                    sems.at[0, d],
                 ),
                 pltpu.make_async_copy(updates[d], upd_v.at[d], sems.at[1, d]),
                 pltpu.make_async_copy(
-                    forcing_ref.at[pl.ds(first, per)], forcing_v.at[d], sems.at[2, d]
+                    forcing_ref.at[pl.ds(group * per, per)], forcing_v.at[d], sems.at[2, d]
                 ),
             ]
         )
@@ -529,14 +556,14 @@
         store.wait()
 
 
-def final_step(place, xt, updates, forcing, cell_mask, layer_scale):
+def final_step(place, halves, updates, forcing, cell_mask, layer_scale):
     slot_count, block_rows, chan_local, block_cols = forcing.shape
     groups = len(updates)
     per = slot_count // groups
     return pl.pallas_call(
-        functools.partial(final_kernel, groups),
+        functools.partial(final_kernel, len(halves), groups),
         out_shape=shape((chan_local, slot_count, block_rows, block_cols)),
-        in_specs=[SMEM] + [ANY] * (groups + 2) + [VMEM, VMEM],
+        in_specs=[SMEM] + [ANY] * (len(halves) + groups + 1) + [VMEM, VMEM],
         out_specs=ANY,
         scratch_shapes=[pltpu.VMEM((groups,) + updates[0].shape, bf16)] * 3
         + [
@@ -545,7 +572,7 @@
         ],
         compiler_params=params(),
         name="final_step",
-    )(place, xt, *updates, forcing, cell_mask, layer_scale.astype(f32)[:, None])
+    )(place, *halves, *updates, forcing, cell_mask, layer_scale.astype(f32)[:, None])
 
 
 def on_device(
@@ -567,32 +594,40 @@
     groups = lax.axis_size(GROUP)
     tile_count = lax.axis_size("tile")
     hid_local = in_weight.shape[1]
-    place = jnp.stack([lax.axis_index(GROUP), lax.axis_index("ens")])
+    place = lax.axis_index(GROUP)[None]
     first_slot = (lax.axis_index("tile") - 1) * slot_count
 
-    xt, strips, packed, part = start_step(
-        place, groups, ocean_state, conv_weight, conv_bias, norm_gain, in_weight, in_bias, out_weight
+    halves, strips, packed, part = start_step(
+        ocean_state, conv_weight, conv_bias, norm_gain, in_weight, in_bias, out_weight
     )
     up = [(i, i + 1) for i in range(tile_count - 1)]
     strips_prev = lax.ppermute(strips, "tile", up)
     strips_next = lax.ppermute(strips, "tile", [(b, a) for a, b in up])
-    parts, starts = exchange_weights(packed, part)
-    bodies = lax.all_to_all(
-        xt.reshape((groups, slot_count // groups) + xt.shape[1:]), GROUP, 0, 0, tiled=True
-    )
+    staged = lax.axis_size("ens") == 2 and lax.axis_size("chan") == 2
+    if staged:
+        near, far, beside, near_beside = exchange_start(packed, part)
+    bodies = spread(halves)
     entries, at = rim_places(neighbours, first_slot, block_rows)
     chosen = onehot_of(at, 3 * block_cols)
     flux = fluxes_of(atmos, flux_weight)
     strips_prev, strips_next, flux = lax.optimization_barrier((strips_prev, strips_next, flux))
     rims = rims_of(place, entries, chosen, strips_prev, strips, strips_next, groups)
+    if staged:
+        far, *rims = lax.optimization_barrier((far, *rims))
     rims = trade(rims)
     table = gather_flux(flux)
+    if staged:
+        parts = [packed, beside, near, far, near_beside, swap(far, "sec")]
+        starts = weight_places()
+    else:
+        parts = [lax.all_gather(packed, GROUP, axis=0, tiled=True)]
+        starts = jnp.zeros((1,), jnp.int32)
     weights = unpack_weights(parts, starts, groups, chan_local, hid_local)
     updates = block_step(place, bodies, rims, weights)
     _, table = lax.optimization_barrier((updates[0], table))
     updates = trade(updates)
     forcing = forcing_of(table, remap, atmos.shape[0], chan_local)
-    return final_step(place, xt, updates, forcing, cell_mask, layer_scale)
+    return final_step(place, halves, updates, forcing, cell_mask, layer_scale)
 
 
 def solution(mesh):

time: 76.7 us -> 82.6 us (1.077)
  the two profiles are of different devices: /device:TPU:0 before, /device:TPU:9 now
where the time goes in v1:
time: 82.6 us; the launch traced here: 82.2 us
  Pallas kernels  28.3 us (34%)
  waiting for transfers between devices  24.4 us (30%)
  starting transfers between devices  23.8 us (29%)
  local copies, waits for them, and re-layouts  3.07 us (4%)
  other arithmetic  2.32 us (3%)
    ppermute x3, waiting for transfers between devices, gather_flux(): pieces.append(lax.ppermute(flux, 'tile', turn))  11.5 us
    pallas_call x1, Pallas kernels, forcing_of(): pl.pallas_call(forcing_kernel, out_shape=shape((slot_count, block_rows, c...  9.71 us
    ppermute x7, starting transfers between devices, swap(): return lax.ppermute(value, axis, [(0, 1), (1, 0)])  9.35 us
    pallas_call x1, Pallas kernels, block_step(): pl.pallas_call(functools.partial(block_kernel, groups), out_shape=(shape(...  8.81 us
    ppermute x7, waiting for transfers between devices, swap(): return lax.ppermute(value, axis, [(0, 1), (1, 0)])  4.89 us
    ppermute x6, starting transfers between devices, send(): return lax.ppermute(piece, GROUP, [(i, i ^ d) for i in range(count)])  4.39 us
    ppermute x1, waiting for transfers between devices, spread(): got[c] = lax.ppermute(halves[c], 'chan', [(i, i ^ c) for i in range(chips)])  4.01 us
    ppermute x6, waiting for transfers between devices, send(): return lax.ppermute(piece, GROUP, [(i, i ^ d) for i in range(count)])  3.92 us
  transfers between devices with their start and end apart: 19, of which 7 were waited for; matrix products, arithmetic and copies ran while one was open for 4% of the time, Pallas kernels for 27%

profile of v1, /device:TPU:9, one launch (start us, length us, event | category | flops | bytes accessed | tf_op | source)
XLA Modules:
  0.0 82.2 jit_solution(17151625751297369558)
XLA Ops:
  0.0 3.9 %start_step.1 = (bf16[8,4,64,128]{3,2,1,0:T(8,128)(2,1)}, bf16[8,4,64,128]{3,2,1,0:T(8,128)(2,1)}, bf16[33,64,128]{2,1,0:T(8,128)(2,1)}, bf16[1120,256]{1,0:T(8,128)(2,1)}, bf16[560,256]{1,0:T(8,128)(2,1)}) custom-call(bf16[64,16,4,128]{3,2,1,0:T(4,128)(2,1)} %refs_0_.1, bf16[9,64,256]{2,1,0:T(8,128)(2,1)} %bitcast.23, bf16[1,64]{1,0:T(2,128)(2,1)} %bitcast.25, ...), custom_call_target="tpu_custom_call" | custom-call | tf_op jit(solution)/shard_map/start_step/pallas_call | solution.py:115
  3.9 3.2 %collective-permute-start.5 = (bf16[33,64,128]{2,1,0:T(8,128)(2,1)}, bf16[33,64,128]{2,1,0:T(8,128)(2,1)}, u32[]{:S(2)}, u32[]{:S(2)}) collective-permute-start(bf16[33,64,128]{2,1,0:T(8,128)(2,1)} %get-tuple-element.42.own_ref), channel_id=1, source_target_pairs={{0,4},{4,8},{8,12},{1,5},{5,9},{9,13},{2,6},{6,10},{10,14},{3,7},{... | collective-permute-start | bytes 1622024 | tf_op jit(solution)/shard_map/ppermute | solution.py:604
  7.1 2.9 %collective-permute-start.6 = (bf16[33,64,128]{2,1,0:T(8,128)(2,1)}, bf16[33,64,128]{2,1,0:T(8,128)(2,1)}, u32[]{:S(2)}, u32[]{:S(2)}) collective-permute-start(bf16[33,64,128]{2,1,0:T(8,128)(2,1)} %get-tuple-element.42.own_ref), channel_id=1, source_target_pairs={{4,0},{8,4},{12,8},{5,1},{9,5},{13,9},{6,2},{10,6},{14,10},{7,3},{... | collective-permute-start | bytes 1622024 | tf_op jit(solution)/shard_map/ppermute | solution.py:605
  10.0 1.3 %collective-permute-start.3 = (bf16[560,256]{1,0:T(8,128)(2,1)}, bf16[560,256]{1,0:T(8,128)(2,1)S(1)}, u32[]{:S(2)}, u32[]{:S(2)}) collective-permute-start(bf16[560,256]{1,0:T(8,128)(2,1)} %get-tuple-element.39), channel_id=1, source_target_pairs={{0,2},{2,0},{1,3},{3,1},{4,6},{6,4},{5,7},{7,5},{8,10},{10,8},{9,1... | collective-permute-start | bytes 860168 | tf_op jit(solution)/shard_map/ppermute | solution.py:206
  11.3 0.3 collective-permute-start.1
  11.6 0.7 multiply_select_fusion
  12.3 0.7 broadcast_compare_fusion
  13.0 4.5 %collective-permute-done.3.refs_2_ = bf16[560,256]{1,0:T(8,128)(2,1)S(1)} collective-permute-done((bf16[560,256]{1,0:T(8,128)(2,1)}, bf16[560,256]{1,0:T(8,128)(2,1)S(1)}, u32[]{:S(2)}, u32[]{:S(2)}) %collective-permute-start.3) | collective-permute-done | bytes 286752 | tf_op jit(solution)/shard_map/ppermute | solution.py:206
  17.5 1.2 %collective-permute-start.4 = (bf16[560,256]{1,0:T(8,128)(2,1)S(1)}, bf16[560,256]{1,0:T(8,128)(2,1)}, u32[]{:S(2)}, u32[]{:S(2)}) collective-permute-start(bf16[560,256]{1,0:T(8,128)(2,1)S(1)} %collective-permute-done.3.refs_2_), channel_id=1, source_target_pairs={{0,16},{16,0},{1,17},{17,1},{2,18},{18,2},{3,19},{19,3},{4,20},{20... | collective-permute-start | bytes 860168 | tf_op jit(solution)/shard_map/ppermute | solution.py:206
  18.7 4.1 %collective-permute-start.10 = (bf16[1120,256]{1,0:T(8,128)(2,1)}, bf16[1120,256]{1,0:T(8,128)(2,1)S(1)}, u32[]{:S(2)}, u32[]{:S(2)}) collective-permute-start(bf16[1120,256]{1,0:T(8,128)(2,1)} %get-tuple-element.53.refs_0_), channel_id=1, source_target_pairs={{0,1},{1,0},{2,3},{3,2},{4,5},{5,4},{6,7},{7,6},{8,9},{9,8},{10,11... | collective-permute-start | bytes 1720328 | tf_op jit(solution)/shard_map/ppermute | solution.py:206
  22.9 0.1 copy.14
  22.9 0.1 copy.15
  23.0 0.1 copy.16
  23.1 0.1 copy.17
  23.2 0.1 copy.18
  23.3 0.1 copy.19
  23.4 0.1 copy.20
  23.4 0.1 copy.21
  23.5 0.1 copy.22
  23.6 0.1 copy.23
  23.7 0.1 copy.24
  23.8 0.1 copy.25
  23.9 0.1 stack.19
  24.0 0.0 copy-start.1
  24.0 0.1 reshape.61.at_ref
  24.1 0.6 fluxes.1
  24.7 4.0 %collective-permute-done.1.refs_2_ = bf16[8,4,64,128]{3,2,1,0:T(8,128)(2,1)} collective-permute-done((bf16[8,4,64,128]{3,2,1,0:T(8,128)(2,1)}, bf16[8,4,64,128]{3,2,1,0:T(8,128)(2,1)}, u32[]{:S(2)}, u32[]{:S(2)}) %collective-permute-start.1) | collective-permute-done | bytes 524320 | tf_op jit(solution)/shard_map/ppermute | solution.py:228
  28.7 2.2 %collective-permute-start = (bf16[8,4,64,128]{3,2,1,0:T(8,128)(2,1)}, bf16[8,4,64,128]{3,2,1,0:T(8,128)(2,1)}, u32[]{:S(2)}, u32[]{:S(2)}) collective-permute-start(bf16[8,4,64,128]{3,2,1,0:T(8,128)(2,1)} %get-tuple-element.37.refs_0_), channel_id=1, source_target_pairs={{0,1},{1,0},{2,3},{3,2},{4,5},{5,4},{6,7},{7,6},{8,9},{9,8},{10,11... | collective-permute-start | bytes 1572872 | tf_op jit(solution)/shard_map/ppermute | solution.py:206
  30.9 0.0 collective-permute-start.11
  30.9 0.5 collective-permute-start.2
  31.4 1.0 %copy-done.2 = bf16[33,64,128]{2,1,0:T(8,128)(2,1)S(1)} copy-done((bf16[33,64,128]{2,1,0:T(8,128)(2,1)S(1)}, bf16[33,64,128]{2,1,0:T(8,128)(2,1)}, u32[]{:S(2)}) %copy-start.2) | copy-done | bytes 540696
  32.5 1.5 %rims.1 = (bf16[9,64,128]{2,1,0:T(8,128)(2,1)S(1)}, bf16[9,64,128]{2,1,0:T(8,128)(2,1)S(1)}, bf16[9,64,128]{2,1,0:T(8,128)(2,1)S(1)}, bf16[9,64,128]{2,1,0:T(8,128)(2,1)S(1)}) custom-call(s32[1]{0:T(128)} %bitcast.place_ref, s32[2,16]{1,0:T(2,128)S(1)} %pad_add_fusion.entry_ref, bf16[384,256]{1,0:T(8,128)(2,1)S(1)} %onehot.1.chosen_ref, ...), custom_call_target="tpu_custom_call" | custom-call | tf_op jit(solution)/shard_map/rims/pallas_call | solution.py:321
  34.0 0.6 copy-done.7
  34.6 0.0 collective-permute-done.4.refs_3_
  34.6 0.1 collective-permute-start.12
  34.7 0.7 bitcast_convert_fusion
  35.4 0.1 copy.26.refs_8_
  35.5 0.1 stack.47.starts_ref
  35.6 0.0 collective-permute-done.11.refs_4_
  35.6 0.5 collective-permute-start.7
  36.0 0.3 collective-permute-done.12.refs_5_
  36.4 1.2 %collective-permute-start.8 = (bf16[9,64,128]{2,1,0:T(8,128)(2,1)S(1)}, bf16[9,64,128]{2,1,0:T(8,128)(2,1)S(1)}, u32[]{:S(2)}, u32[]{:S(2)}) collective-permute-start(bf16[9,64,128]{2,1,0:T(8,128)(2,1)S(1)} %get-tuple-element.51), channel_id=1, source_target_pairs={{0,2},{1,3},{2,0},{3,1},{4,6},{5,7},{6,4},{7,5},{8,10},{9,11},{10,... | collective-permute-start | bytes 442376 | tf_op jit(solution)/shard_map/ppermute | solution.py:146
  37.6 0.0 collective-permute-done.10.refs_1_
  37.6 0.6 collective-permute-start.9
  38.2 0.1 add_select_fusion
  38.2 1.5 %unpack_weights.1 = (bf16[256,2304]{1,0:T(8,128)(2,1)S(1)}, bf16[1024,256]{1,0:T(8,128)(2,1)S(1)}, bf16[256,1024]{1,0:T(8,128)(2,1)S(1)}, f32[256,32]{1,0:T(8,128)S(1)}, f32[1024,32]{1,0:T(8,128)S(1)}) custom-call(s32[6]{0:T(128)S(1)} %stack.47.starts_ref, bf16[1120,256]{1,0:T(8,128)(2,1)S(1)} %copy-done.1, ...), custom_call_target="tpu_custom_call" | custom-call | tf_op jit(solution)/shard_map/unpack_weights/pallas_call | solution.py:188
  39.8 0.0 collective-permute-done.refs_1_
  39.8 0.6 collective-permute-start.16
  40.4 1.8 %collective-permute-start.17 = (bf16[1024,128]{1,0:T(8,128)(2,1)S(1)}, bf16[1024,128]{1,0:T(8,128)(2,1)S(1)}, u32[]{:S(2)}, u32[]{:S(2)}) collective-permute-start(bf16[1024,128]{1,0:T(8,128)(2,1)S(1)} %fluxes.1), channel_id=1, source_target_pairs={{0,8},{4,12},{8,0},{12,4},{1,9},{5,13},{9,1},{13,5},{2,10},{6,14},... | collective-permute-start | bytes 786440 | tf_op jit(solution)/shard_map/ppermute | solution.py:484
  42.2 0.0 collective-permute-done.8.refs_6_
  42.2 1.4 %collective-permute-start.18 = (bf16[1024,128]{1,0:T(8,128)(2,1)S(1)}, bf16[1024,128]{1,0:T(8,128)(2,1)S(1)}, u32[]{:S(2)}, u32[]{:S(2)}) collective-permute-start(bf16[1024,128]{1,0:T(8,128)(2,1)S(1)} %fluxes.1), channel_id=1, source_target_pairs={{0,12},{4,0},{8,4},{12,8},{1,13},{5,1},{9,5},{13,9},{2,14},{6,2},{... | collective-permute-start | bytes 786440 | tf_op jit(solution)/shard_map/ppermute | solution.py:484
  43.6 1.8 %collective-permute-done.9.refs_7_ = bf16[9,64,128]{2,1,0:T(8,128)(2,1)S(1)} collective-permute-done((bf16[9,64,128]{2,1,0:T(8,128)(2,1)}, bf16[9,64,128]{2,1,0:T(8,128)(2,1)S(1)}, u32[]{:S(2)}, u32[]{:S(2)}) %collective-permute-start.9) | collective-permute-done | bytes 147488 | tf_op jit(solution)/shard_map/ppermute | solution.py:146
  45.4 8.8 %block_step.1 = (bf16[4,4,64,128]{3,2,1,0:T(8,128)(2,1)S(1)}, bf16[4,4,64,128]{3,2,1,0:T(8,128)(2,1)S(1)}, bf16[4,4,64,128]{3,2,1,0:T(8,128)(2,1)S(1)}, bf16[4,4,64,128]{3,2,1,0:T(8,128)(2,1)S(1)}) custom-call(s32[1]{0:T(128)} %bitcast.place_ref, bf16[8,4,64,128]{3,2,1,0:T(8,128)(2,1)S(1)} %copy-done.3, ...), custom_call_target="tpu_custom_call" | custom-call | flops 4563402752 | bytes 8388608 | tf_op jit(solution)/shard_map/block_step/pallas_call | solution.py:416
  54.2 8.6 %collective-permute-done.17 = bf16[1024,128]{1,0:T(8,128)(2,1)S(1)} collective-permute-done((bf16[1024,128]{1,0:T(8,128)(2,1)S(1)}, bf16[1024,128]{1,0:T(8,128)(2,1)S(1)}, u32[]{:S(2)}, u32[]{:S(2)}) %collective-permute-start.17) | collective-permute-done | bytes 262176 | tf_op jit(solution)/shard_map/ppermute | solution.py:484
  62.9 2.9 %collective-permute-done.18 = bf16[1024,128]{1,0:T(8,128)(2,1)S(1)} collective-permute-done((bf16[1024,128]{1,0:T(8,128)(2,1)S(1)}, bf16[1024,128]{1,0:T(8,128)(2,1)S(1)}, u32[]{:S(2)}, u32[]{:S(2)}) %collective-permute-start.18) | collective-permute-done | bytes 262176 | tf_op jit(solution)/shard_map/ppermute | solution.py:484
  65.8 0.5 collective-permute-start.13
  66.2 1.2 %collective-permute-start.14 = (bf16[4,4,64,128]{3,2,1,0:T(8,128)(2,1)S(1)}, bf16[4,4,64,128]{3,2,1,0:T(8,128)(2,1)S(1)}, u32[]{:S(2)}, u32[]{:S(2)}) collective-permute-start(bf16[4,4,64,128]{3,2,1,0:T(8,128)(2,1)S(1)} %get-tuple-element.62), channel_id=1, source_target_pairs={{0,2},{1,3},{2,0},{3,1},{4,6},{5,7},{6,4},{7,5},{8,10},{9,11},{10,... | collective-permute-start | bytes 786440 | tf_op jit(solution)/shard_map/ppermute | solution.py:146
  67.5 0.5 collective-permute-start.15
  67.9 0.1 maximum_convert_fusion
  68.1 0.0 copy-start.6
  68.1 9.7 %forcing.1.refs_6_ = bf16[16,4,64,128]{3,2,1,0:T(8,128)(2,1)S(1)} custom-call(s32[64,128]{1,0:T(8,128)S(1)} %get-tuple-element.70.row_ref, s32[64,128]{1,0:T(8,128)S(1)} %get-tuple-element.69.side_ref, f32[4096,1,128]{2,1,0:T(1,128)S(1)} %bitcast.21), custom_call_target="tpu_custom_call" | custom-call | bytes 33554432 | tf_op jit(solution)/shard_map/forcing/pallas_call | solution.py:501
  77.8 0.0 collective-permute-done.14.refs_4_
  77.8 2.1 %collective-permute-done.15.refs_5_ = bf16[4,4,64,128]{3,2,1,0:T(8,128)(2,1)S(1)} collective-permute-done((bf16[4,4,64,128]{3,2,1,0:T(8,128)(2,1)S(1)}, bf16[4,4,64,128]{3,2,1,0:T(8,128)(2,1)S(1)}, u32[]{:S(2)}, u32[]{:S(2)}) %collective-permute-start.15) | collective-permute-done | bytes 262176 | tf_op jit(solution)/shard_map/ppermute | solution.py:146
  79.9 2.2 %final_step.1 = bf16[64,16,4,128]{3,2,1,0:T(4,128)(2,1)} custom-call(s32[1]{0:T(128)} %bitcast.place_ref, bf16[8,4,64,128]{3,2,1,0:T(8,128)(2,1)S(1)} %copy-done.3, bf16[8,4,64,128]{3,2,1,0:T(8,128)(2,1)S(1)} %copy-done.4, bf16[4,4,64,128]{3,2,1,0:T(8,128)(2,1)S(1)} %get-tuple-element.60.refs_2_, ...), custom_call_target="tpu_custom_call" | custom-call | tf_op jit(solution)/shard_map/final_step/pallas_call | solution.py:563
  (25 shorter events, 0.1 us)
Async XLA Ops:
  0.0 24.1 %copy-start.5 = (bf16[384,64]{0,1:T(8,128)(2,1)S(1)}, bf16[384,64]{0,1:T(8,128)(2,1)}, u32[]{:S(2)}) copy-start(bf16[384,64]{0,1:T(8,128)(2,1)} %param.15) | copy-start | bytes 147460
  0.0 24.1 %copy-start = (bf16[2048,384]{1,0:T(8,128)(2,1)S(1)}, bf16[2048,384]{1,0:T(8,128)(2,1)}, u32[]{:S(2)}) copy-start(bf16[2048,384]{1,0:T(8,128)(2,1)} %atmos_ref.1) | copy-start | bytes 4718596
  3.9 27.0 %collective-permute-start.5 = (bf16[33,64,128]{2,1,0:T(8,128)(2,1)}, bf16[33,64,128]{2,1,0:T(8,128)(2,1)}, u32[]{:S(2)}, u32[]{:S(2)}) collective-permute-start(bf16[33,64,128]{2,1,0:T(8,128)(2,1)} %get-tuple-element.42.own_ref), channel_id=1, source_target_pairs={{0,4},{4,8},{8,12},{1,5},{5,9},{9,13},{2,6},{6,10},{10,14},{3,7},{... | collective-permute-start | bytes 1622024 | tf_op jit(solution)/shard_map/ppermute | solution.py:604
  7.1 23.8 %collective-permute-start.6 = (bf16[33,64,128]{2,1,0:T(8,128)(2,1)}, bf16[33,64,128]{2,1,0:T(8,128)(2,1)}, u32[]{:S(2)}, u32[]{:S(2)}) collective-permute-start(bf16[33,64,128]{2,1,0:T(8,128)(2,1)} %get-tuple-element.42.own_ref), channel_id=1, source_target_pairs={{4,0},{8,4},{12,8},{5,1},{9,5},{13,9},{6,2},{10,6},{14,10},{7,3},{... | collective-permute-start | bytes 1622024 | tf_op jit(solution)/shard_map/ppermute | solution.py:605
  10.0 7.5 %collective-permute-start.3 = (bf16[560,256]{1,0:T(8,128)(2,1)}, bf16[560,256]{1,0:T(8,128)(2,1)S(1)}, u32[]{:S(2)}, u32[]{:S(2)}) collective-permute-start(bf16[560,256]{1,0:T(8,128)(2,1)} %get-tuple-element.39), channel_id=1, source_target_pairs={{0,2},{2,0},{1,3},{3,1},{4,6},{6,4},{5,7},{7,5},{8,10},{10,8},{9,1... | collective-permute-start | bytes 860168 | tf_op jit(solution)/shard_map/ppermute | solution.py:206
  11.3 17.4 %collective-permute-start.1 = (bf16[8,4,64,128]{3,2,1,0:T(8,128)(2,1)}, bf16[8,4,64,128]{3,2,1,0:T(8,128)(2,1)}, u32[]{:S(2)}, u32[]{:S(2)}) collective-permute-start(bf16[8,4,64,128]{3,2,1,0:T(8,128)(2,1)} %get-tuple-element.38.refs_1_), channel_id=1, source_target_pairs={{0,2},{2,0},{1,3},{3,1},{4,6},{6,4},{5,7},{7,5},{8,10},{10,8},{9,1... | collective-permute-start | bytes 1572872 | tf_op jit(solution)/shard_map/ppermute | solution.py:228
  17.5 17.1 %collective-permute-start.4 = (bf16[560,256]{1,0:T(8,128)(2,1)S(1)}, bf16[560,256]{1,0:T(8,128)(2,1)}, u32[]{:S(2)}, u32[]{:S(2)}) collective-permute-start(bf16[560,256]{1,0:T(8,128)(2,1)S(1)} %collective-permute-done.3.refs_2_), channel_id=1, source_target_pairs={{0,16},{16,0},{1,17},{17,1},{2,18},{18,2},{3,19},{19,3},{4,20},{20... | collective-permute-start | bytes 860168 | tf_op jit(solution)/shard_map/ppermute | solution.py:206
  18.7 18.9 %collective-permute-start.10 = (bf16[1120,256]{1,0:T(8,128)(2,1)}, bf16[1120,256]{1,0:T(8,128)(2,1)S(1)}, u32[]{:S(2)}, u32[]{:S(2)}) collective-permute-start(bf16[1120,256]{1,0:T(8,128)(2,1)} %get-tuple-element.53.refs_0_), channel_id=1, source_target_pairs={{0,1},{1,0},{2,3},{3,2},{4,5},{5,4},{6,7},{7,6},{8,9},{9,8},{10,11... | collective-permute-start | bytes 1720328 | tf_op jit(solution)/shard_map/ppermute | solution.py:206
  23.6 11.9 %copy-start.8 = (s32[16,4,128]{2,1,0:T(4,128)S(1)}, s32[16,4,128]{2,1,0:T(4,128)}, u32[]{:S(2)}) copy-start(s32[16,4,128]{2,1,0:T(4,128)} %param.25) | copy-start | bytes 98308
  24.0 14.3 %copy-start.1 = (bf16[1120,256]{1,0:T(8,128)(2,1)S(1)}, bf16[1120,256]{1,0:T(8,128)(2,1)}, u32[]{:S(2)}) copy-start(bf16[1120,256]{1,0:T(8,128)(2,1)} %get-tuple-element.53.refs_0_) | copy-start | bytes 1720324
  28.7 11.1 %collective-permute-start = (bf16[8,4,64,128]{3,2,1,0:T(8,128)(2,1)}, bf16[8,4,64,128]{3,2,1,0:T(8,128)(2,1)}, u32[]{:S(2)}, u32[]{:S(2)}) collective-permute-start(bf16[8,4,64,128]{3,2,1,0:T(8,128)(2,1)} %get-tuple-element.37.refs_0_), channel_id=1, source_target_pairs={{0,1},{1,0},{2,3},{3,2},{4,5},{5,4},{6,7},{7,6},{8,9},{9,8},{10,11... | collective-permute-start | bytes 1572872 | tf_op jit(solution)/shard_map/ppermute | solution.py:206
  30.9 4.7 %collective-permute-start.11 = (bf16[560,256]{1,0:T(8,128)(2,1)S(1)}, bf16[560,256]{1,0:T(8,128)(2,1)}, u32[]{:S(2)}, u32[]{:S(2)}) collective-permute-start(bf16[560,256]{1,0:T(8,128)(2,1)S(1)} %collective-permute-done.3.refs_2_), channel_id=1, source_target_pairs={{0,1},{1,0},{2,3},{3,2},{4,5},{5,4},{6,7},{7,6},{8,9},{9,8},{10,11... | collective-permute-start | bytes 860168 | tf_op jit(solution)/shard_map/ppermute | solution.py:206
  30.9 14.5 %collective-permute-start.2 = (bf16[8,4,64,128]{3,2,1,0:T(8,128)(2,1)}, bf16[8,4,64,128]{3,2,1,0:T(8,128)(2,1)}, u32[]{:S(2)}, u32[]{:S(2)}) collective-permute-start(bf16[8,4,64,128]{3,2,1,0:T(8,128)(2,1)} %collective-permute-done.1.refs_2_), channel_id=1, source_target_pairs={{0,1},{1,0},{2,3},{3,2},{4,5},{5,4},{6,7},{7,6},{8,9},{9,8},{10,11... | collective-permute-start | bytes 1572872 | tf_op jit(solution)/shard_map/ppermute | solution.py:206
  31.4 1.0 %copy-start.2 = (bf16[33,64,128]{2,1,0:T(8,128)(2,1)S(1)}, bf16[33,64,128]{2,1,0:T(8,128)(2,1)}, u32[]{:S(2)}) copy-start(bf16[33,64,128]{2,1,0:T(8,128)(2,1)} %get-tuple-element.42.own_ref) | copy-start | bytes 1622020
  33.9 0.7 copy-start.7
  34.6 10.8 %copy-start.3 = (bf16[8,4,64,128]{3,2,1,0:T(8,128)(2,1)S(1)}, bf16[8,4,64,128]{3,2,1,0:T(8,128)(2,1)}, u32[]{:S(2)}) copy-start(bf16[8,4,64,128]{3,2,1,0:T(8,128)(2,1)} %get-tuple-element.37.refs_0_) | copy-start | bytes 1572868
  34.6 1.8 %collective-permute-start.12 = (bf16[560,256]{1,0:T(8,128)(2,1)}, bf16[560,256]{1,0:T(8,128)(2,1)S(1)}, u32[]{:S(2)}, u32[]{:S(2)}) collective-permute-start(bf16[560,256]{1,0:T(8,128)(2,1)} %collective-permute-done.4.refs_3_), channel_id=1, source_target_pairs={{0,1},{1,0},{2,3},{3,2},{4,5},{5,4},{6,7},{7,6},{8,9},{9,8},{10,11... | collective-permute-start | bytes 860168 | tf_op jit(solution)/shard_map/ppermute | solution.py:206
  35.6 4.8 %collective-permute-start.7 = (bf16[9,64,128]{2,1,0:T(8,128)(2,1)S(1)}, bf16[9,64,128]{2,1,0:T(8,128)(2,1)S(1)}, u32[]{:S(2)}, u32[]{:S(2)}) collective-permute-start(bf16[9,64,128]{2,1,0:T(8,128)(2,1)S(1)} %get-tuple-element.50), channel_id=1, source_target_pairs={{0,1},{1,0},{2,3},{3,2},{4,5},{5,4},{6,7},{7,6},{8,9},{9,8},{10,11... | collective-permute-start | bytes 442376 | tf_op jit(solution)/shard_map/ppermute | solution.py:146
  36.4 5.8 %collective-permute-start.8 = (bf16[9,64,128]{2,1,0:T(8,128)(2,1)S(1)}, bf16[9,64,128]{2,1,0:T(8,128)(2,1)S(1)}, u32[]{:S(2)}, u32[]{:S(2)}) collective-permute-start(bf16[9,64,128]{2,1,0:T(8,128)(2,1)S(1)} %get-tuple-element.51), channel_id=1, source_target_pairs={{0,2},{1,3},{2,0},{3,1},{4,6},{5,7},{6,4},{7,5},{8,10},{9,11},{10,... | collective-permute-start | bytes 442376 | tf_op jit(solution)/shard_map/ppermute | solution.py:146
  37.6 7.8 %collective-permute-start.9 = (bf16[9,64,128]{2,1,0:T(8,128)(2,1)}, bf16[9,64,128]{2,1,0:T(8,128)(2,1)S(1)}, u32[]{:S(2)}, u32[]{:S(2)}) collective-permute-start(bf16[9,64,128]{2,1,0:T(8,128)(2,1)} %copy-done.7), channel_id=1, source_target_pairs={{0,3},{1,2},{2,1},{3,0},{4,7},{5,6},{6,5},{7,4},{8,11},{9,10},{10,... | collective-permute-start | bytes 442376 | tf_op jit(solution)/shard_map/ppermute | solution.py:146
  39.8 14.4 %collective-permute-start.16 = (bf16[1024,128]{1,0:T(8,128)(2,1)S(1)}, bf16[1024,128]{1,0:T(8,128)(2,1)S(1)}, u32[]{:S(2)}, u32[]{:S(2)}) collective-permute-start(bf16[1024,128]{1,0:T(8,128)(2,1)S(1)} %fluxes.1), channel_id=1, source_target_pairs={{0,4},{4,8},{8,12},{12,0},{1,5},{5,9},{9,13},{13,1},{2,6},{6,10},{... | collective-permute-start | bytes 786440 | tf_op jit(solution)/shard_map/ppermute | solution.py:484
  40.4 22.5 %collective-permute-start.17 = (bf16[1024,128]{1,0:T(8,128)(2,1)S(1)}, bf16[1024,128]{1,0:T(8,128)(2,1)S(1)}, u32[]{:S(2)}, u32[]{:S(2)}) collective-permute-start(bf16[1024,128]{1,0:T(8,128)(2,1)S(1)} %fluxes.1), channel_id=1, source_target_pairs={{0,8},{4,12},{8,0},{12,4},{1,9},{5,13},{9,1},{13,5},{2,10},{6,14},... | collective-permute-start | bytes 786440 | tf_op jit(solution)/shard_map/ppermute | solution.py:484
  42.2 23.6 %collective-permute-start.18 = (bf16[1024,128]{1,0:T(8,128)(2,1)S(1)}, bf16[1024,128]{1,0:T(8,128)(2,1)S(1)}, u32[]{:S(2)}, u32[]{:S(2)}) collective-permute-start(bf16[1024,128]{1,0:T(8,128)(2,1)S(1)} %fluxes.1), channel_id=1, source_target_pairs={{0,12},{4,0},{8,4},{12,8},{1,13},{5,1},{9,5},{13,9},{2,14},{6,2},{... | collective-permute-start | bytes 786440 | tf_op jit(solution)/shard_map/ppermute | solution.py:484
  65.8 12.0 %collective-permute-start.13 = (bf16[4,4,64,128]{3,2,1,0:T(8,128)(2,1)S(1)}, bf16[4,4,64,128]{3,2,1,0:T(8,128)(2,1)S(1)}, u32[]{:S(2)}, u32[]{:S(2)}) collective-permute-start(bf16[4,4,64,128]{3,2,1,0:T(8,128)(2,1)S(1)} %get-tuple-element.61), channel_id=1, source_target_pairs={{0,1},{1,0},{2,3},{3,2},{4,5},{5,4},{6,7},{7,6},{8,9},{9,8},{10,11... | collective-permute-start | bytes 786440 | tf_op jit(solution)/shard_map/ppermute | solution.py:146
  66.2 11.6 %collective-permute-start.14 = (bf16[4,4,64,128]{3,2,1,0:T(8,128)(2,1)S(1)}, bf16[4,4,64,128]{3,2,1,0:T(8,128)(2,1)S(1)}, u32[]{:S(2)}, u32[]{:S(2)}) collective-permute-start(bf16[4,4,64,128]{3,2,1,0:T(8,128)(2,1)S(1)} %get-tuple-element.62), channel_id=1, source_target_pairs={{0,2},{1,3},{2,0},{3,1},{4,6},{5,7},{6,4},{7,5},{8,10},{9,11},{10,... | collective-permute-start | bytes 786440 | tf_op jit(solution)/shard_map/ppermute | solution.py:146
  67.5 12.4 %collective-permute-start.15 = (bf16[4,4,64,128]{3,2,1,0:T(8,128)(2,1)S(1)}, bf16[4,4,64,128]{3,2,1,0:T(8,128)(2,1)S(1)}, u32[]{:S(2)}, u32[]{:S(2)}) collective-permute-start(bf16[4,4,64,128]{3,2,1,0:T(8,128)(2,1)S(1)} %get-tuple-element.63), channel_id=1, source_target_pairs={{0,3},{1,2},{2,1},{3,0},{4,7},{5,6},{6,5},{7,4},{8,11},{9,10},{10,... | collective-permute-start | bytes 786440 | tf_op jit(solution)/shard_map/ppermute | solution.py:146
  68.1 11.8 %copy-start.4 = (bf16[8,4,64,128]{3,2,1,0:T(8,128)(2,1)S(1)}, bf16[8,4,64,128]{3,2,1,0:T(8,128)(2,1)}, u32[]{:S(2)}) copy-start(bf16[8,4,64,128]{3,2,1,0:T(8,128)(2,1)} %get-tuple-element.38.refs_1_) | copy-start | bytes 1572868
  68.1 11.8 %copy-start.6 = (s32[16,4,128]{2,1,0:T(4,128)S(1)}, s32[16,4,128]{2,1,0:T(4,128)}, u32[]{:S(2)}) copy-start(s32[16,4,128]{2,1,0:T(4,128)} %refs_7_.1) | copy-start | bytes 98308
